TPU v7x, 32 devices: a whole 2x2x4 slice. The times are simulated.
32 devices in a mesh: lat: 8 (over z, y), tok: 4 (over x, core).
Axes of the slice: x: 2, y: 2, z: 4, core: 2. Of those that a mesh axis runs over, the one named last changes fastest.
Arguments:
- resid: bfloat16 [8192, 512], P('lat', 'tok'), may hold values from -6 to 6
- active_ids: int32 [512, 64], P('tok'), may hold values from 0 to 16383, all different within a row
- w_enc: bfloat16 [16384, 8192], P('lat', 'tok'), may hold values from -0.5 to 0.5
- w_dec: bfloat16 [16384, 8192], P('lat', 'tok'), may hold values from -0.0625 to 0.0625
- b_enc: float32 [16384], P('lat'), may hold values from -8 to 8
- b_dec: bfloat16 [8192], P('lat'), may hold values from -3 to 3
Outputs:
- grad_w_enc: bfloat16 [16384, 8192], P('lat', 'tok')
- grad_w_dec: bfloat16 [16384, 8192], P('lat', 'tok')
- grad_b_enc: float32 [16384], P('lat')
- grad_b_dec: float32 [8192], P('tok')
Inputs may be any that keep to these rules, and one draw needn't show every extreme that they name: `active_ids`: the 64 latents of a token are distinct, and every latent is active for some token.
All inputs are finite; a program needn't handle non-finite values.
Results may differ from a plain program's by a relative error of at most 0.0068.
Values may be sent and summed in bfloat16 or wider, within the bound.
A program may use at most 256 MiB of HBM per device.

v0:
```python
import jax
import jax.numpy as jnp
from jax import lax
from jax.sharding import PartitionSpec as P

f32 = jnp.float32
bf16 = jnp.bfloat16


def active_rows(ids, base, rows):
    word = 32 if rows % 32 == 0 else rows
    local = ids - base
    which = local // word
    place = local - which * word
    bit = lax.shift_left(jnp.int32(1), place)
    words = lax.iota(jnp.int32, rows // word)
    held = jnp.where(which[None, :, :] == words[:, None, None], bit[None, :, :], 0)
    held = jnp.sum(held, axis=1)
    shifts = lax.iota(jnp.int32, word)
    flags = lax.shift_right_logical(held[:, None, :], jnp.broadcast_to(shifts[None, :, None], (rows // word, word, held.shape[1]))) & 1
    return flags.reshape(rows, held.shape[1]).astype(f32)


def on_device(resid, active_ids, w_enc, w_dec, b_enc, b_dec):
    block_rows = w_enc.shape[0]
    width = w_enc.shape[1]
    lat_pos = lax.axis_index("lat")
    tok_pos = lax.axis_index("tok")
    tok_count = lax.axis_size("tok")
    lat_count = lax.axis_size("lat")
    rows = block_rows // tok_count
    feats = width // lat_count

    ids_all = lax.all_gather(active_ids, "tok", axis=0, tiled=True).T
    bias_full = lax.all_gather(b_dec, "lat", axis=0, tiled=True)
    resid_full = lax.all_gather(resid, "lat", axis=0, tiled=True)
    resid_mine = lax.all_to_all(resid_full, "tok", split_axis=0, concat_axis=1, tiled=True)
    bias_mine = lax.dynamic_slice_in_dim(bias_full, tok_pos * width, width, 0)
    centred = (resid_mine.astype(f32) - bias_mine.astype(f32)[:, None]).astype(bf16)

    active = active_rows(ids_all, lat_pos * block_rows + tok_pos * rows, rows)
    b_rows = lax.dynamic_slice_in_dim(b_enc, tok_pos * rows, rows, 0)

    pre_part = jnp.dot(w_enc, centred, preferred_element_type=f32).astype(bf16)
    pre = lax.psum_scatter(pre_part, "tok", scatter_dimension=0, tiled=True)
    codes_rows = ((pre.astype(f32) + b_rows[:, None]) * active).astype(bf16)
    codes = lax.all_gather(codes_rows, "tok", axis=0, tiled=True)

    recon_part = lax.dot_general(
        w_dec, codes, (((0,), (0,)), ((), ())), preferred_element_type=f32
    ).astype(bf16)
    recon = lax.psum_scatter(recon_part, "lat", scatter_dimension=0, tiled=True)
    r_rows = lax.dynamic_slice_in_dim(resid_mine, lat_pos * feats, feats, 0)
    bd_rows = lax.dynamic_slice_in_dim(bias_mine, lat_pos * feats, feats, 0)
    error_rows = (
        recon.astype(f32) + bd_rows.astype(f32)[:, None] - r_rows.astype(f32)
    ).astype(bf16)
    errors = lax.all_gather(error_rows, "lat", axis=0, tiled=True)

    gc_part = jnp.dot(w_dec, errors, preferred_element_type=f32).astype(bf16)
    gc = lax.psum_scatter(gc_part, "tok", scatter_dimension=0, tiled=True)
    gp_rows = (gc.astype(f32) * active).astype(bf16)
    grad_pre = lax.all_gather(gp_rows, "tok", axis=0, tiled=True)

    grad_w_dec = lax.dot_general(
        codes, errors, (((1,), (1,)), ((), ())), preferred_element_type=f32
    ).astype(bf16)
    grad_b_enc = jnp.sum(grad_pre.astype(f32), axis=1)
    high = grad_b_enc.astype(bf16)
    rest = grad_b_enc - high.astype(f32)
    mid = rest.astype(bf16)
    low = (rest - mid.astype(f32)).astype(bf16)
    parts = jnp.stack([high, mid, low])
    back = jnp.sum(jnp.dot(parts, w_enc, preferred_element_type=f32), axis=0)
    back = lax.psum(back, "lat")
    error_total = jnp.sum(errors.astype(f32), axis=1)
    grad_w_enc = lax.dot_general(
        grad_pre, centred, (((1,), (1,)), ((), ())), preferred_element_type=f32
    ).astype(bf16)
    return (grad_w_enc, grad_w_dec, grad_b_enc, error_total - back)


def solution(mesh):
    return jax.shard_map(
        on_device,
        mesh=mesh,
        in_specs=(
            P("lat", "tok"),
            P("tok", None),
            P("lat", "tok"),
            P("lat", "tok"),
            P("lat"),
            P("lat"),
        ),
        out_specs=(P("lat", "tok"), P("lat", "tok"), P("lat"), P("tok")),
        check_vma=False,
    )
```

profile of v0, /device:TPU:0, one launch (start us, length us, event | category | flops | bytes accessed | tf_op | source)
XLA Modules:
  0.0 399.6 jit_solution(10416619332048094439)
XLA Ops:
  7.2 0.0 all-gather.5.cloned.1.call-start
  7.2 0.7 all-gather.5.cloned.1.call-update
  7.9 54.2 %all-gather.5.cloned.1.call-done = bf16[8192,128]{1,0:T(8,128)(2,1)} async-done(((bf16[1024,128]{1,0:T(8,128)(2,1)}), bf16[8192,128]{1,0:T(8,128)(2,1)}) %all-gather.5.cloned.1.call-update) | async-done | bytes 2097168 | tf_op jit(solution)/shard_map/all_gather | solution.py:36
  62.1 3.9 copy.15
  66.1 0.0 copy-start.5
  66.1 3.7 all-to-all-start
  69.8 0.0 reduce-scatter.4.cloned.1.call-start
  69.9 0.0 copy-done.5
  69.9 26.0 %all_gather.19 = bf16[8192]{0:T(1024)(128)(2,1)S(1)} all-gather(bf16[1024]{0:T(1024)(128)(2,1)S(1)} %copy-done.5), channel_id=1, replica_groups=mesh['lat'=8,'tok'=4] {'lat'}, dimensions={0}, use_global_device_ids=true | all-gather | bytes 18432 | tf_op jit(solution)/shard_map/all_gather | solution.py:35
  95.9 0.0 all-to-all-done
  95.9 0.0 copy-start
  95.9 9.9 %fusion = bf16[2048,512]{0,1:T(8,128)(2,1)} fusion(bf16[2048,2048]{1,0:T(8,128)(2,1)} %param.8, bf16[2048,512]{0,1:T(8,128)(2,1)S(1)} %bitcast.43, f32[2048]{0:T(1024)S(1)} %dynamic-slice_convert_fusion), kind=kOutput, calls=%fused_computation.8 | convolution fusion | flops 4299161600 | bytes 12591104 | tf_op jit(solution)/shard_map/dot_general | solution.py:44
  105.8 0.0 copy-done
  105.8 0.0 copy-start.4
  105.8 0.0 reduce-scatter.4.cloned.1.call-update
  105.8 0.0 all-gather.7.cloned.1.call-start
  105.9 0.1 broadcast_in_dim.32
  106.0 0.6 copy-done.4
  106.5 5.5 %all_gather.20 = s32[512,64]{0,1:T(8,128)S(1)} all-gather(s32[128,64]{0,1:T(8,128)S(1)} %copy-done.4), channel_id=1, replica_groups=mesh['lat'=8,'tok'=4] {'tok'}, dimensions={0}, use_global_device_ids=true | all-gather | bytes 163840 | tf_op jit(solution)/shard_map/all_gather | solution.py:34
  112.0 0.1 add_select_fusion
  112.1 0.3 select_reduce_fusion
  112.4 0.1 shift_right_logical.11
  112.5 0.3 copy.16
  112.8 0.8 dynamic_slice.15
  113.6 21.5 %reduce-scatter.4.cloned.1.call-done = bf16[512,512]{0,1:T(8,128)(2,1)} async-done(((bf16[2048,512]{0,1:T(8,128)(2,1)}), bf16[512,512]{0,1:T(8,128)(2,1)}) %reduce-scatter.4.cloned.1.call-update) | async-done | bytes 524304 | tf_op jit(solution)/shard_map/reduce_scatter | solution.py:45
  135.1 2.1 multiply_convert_fusion.1
  137.1 0.0 all-gather.7.cloned.1.call-update
  137.2 0.0 reduce-scatter.6.cloned.1.call-start
  137.2 22.7 %all-gather.7.cloned.1.call-done = bf16[2048,512]{0,1:T(8,128)(2,1)} async-done(((bf16[512,512]{0,1:T(8,128)(2,1)}), bf16[2048,512]{0,1:T(8,128)(2,1)}) %all-gather.7.cloned.1.call-update) | async-done | bytes 2097168 | tf_op jit(solution)/shard_map/all_gather | solution.py:47
  159.9 9.8 %fusion.1 = bf16[2048,512]{0,1:T(8,128)(2,1)} fusion(bf16[2048,512]{0,1:T(8,128)(2,1)} %all-gather.7.cloned.1.call-done, bf16[2048,2048]{1,0:T(8,128)(2,1)} %param.9), kind=kOutput, calls=%fused_computation.9 | convolution fusion | flops 4296015872 | bytes 12582912 | tf_op jit(solution)/shard_map/dot_general | solution.py:49
  169.8 0.0 copy-start.1
  169.8 0.0 reduce-scatter.6.cloned.1.call-update
  169.8 0.0 all-gather.9.cloned.1.call-start
  169.9 0.1 dynamic-slice_convert_fusion.1
  169.9 68.3 %reduce-scatter.6.cloned.1.call-done = bf16[256,512]{0,1:T(8,128)(2,1)} async-done(((bf16[2048,512]{0,1:T(8,128)(2,1)}), bf16[256,512]{0,1:T(8,128)(2,1)}) %reduce-scatter.6.cloned.1.call-update) | async-done | bytes 262160 | tf_op jit(solution)/shard_map/reduce_scatter | solution.py:52
  238.2 0.0 copy-done.1
  238.2 1.7 subtract_convert_fusion.3
  240.0 0.0 all-gather.9.cloned.1.call-update
  240.0 0.0 reduce-scatter.8.cloned.1.call-start
  240.1 51.0 %all-gather.9.cloned.1.call-done = bf16[2048,512]{0,1:T(8,128)(2,1)} async-done(((bf16[256,512]{0,1:T(8,128)(2,1)}), bf16[2048,512]{0,1:T(8,128)(2,1)}) %all-gather.9.cloned.1.call-update) | async-done | bytes 2097168 | tf_op jit(solution)/shard_map/all_gather | solution.py:58
  291.1 9.9 %fusion.2 = bf16[2048,512]{0,1:T(8,128)(2,1)} fusion(bf16[2048,512]{0,1:T(8,128)(2,1)} %all-gather.9.cloned.1.call-done, bf16[2048,2048]{1,0:T(8,128)(2,1)} %param.9), kind=kOutput, calls=%fused_computation.10 | convolution fusion | flops 4296015872 | bytes 12582912 | tf_op jit(solution)/shard_map/dot_general | solution.py:60
  301.0 0.0 reduce-scatter.8.cloned.1.call-update
  301.0 0.2 all-gather.11.cloned.1.call-start
  301.2 29.5 %reduce-scatter.8.cloned.1.call-done = bf16[512,512]{0,1:T(8,128)(2,1)} async-done(((bf16[2048,512]{0,1:T(8,128)(2,1)}), bf16[512,512]{0,1:T(8,128)(2,1)}) %reduce-scatter.8.cloned.1.call-update) | async-done | bytes 524304 | tf_op jit(solution)/shard_map/reduce_scatter | solution.py:61
  330.7 2.0 multiply_convert_fusion
  332.8 0.0 all-gather.11.cloned.1.call-update
  332.8 0.0 copy-start.2
  332.8 2.1 convert_reduce_fusion
  334.9 0.1 copy-done.2
  335.0 8.4 %convolution_convert_fusion = bf16[2048,2048]{1,0:T(8,128)(2,1)} fusion(bf16[2048,512]{0,1:T(8,128)(2,1)} %all-gather.7.cloned.1.call-done, bf16[2048,512]{0,1:T(8,128)(2,1)S(1)} %copy-done.2), kind=kOutput, calls=%fused_computation | convolution fusion | flops 4299161600 | bytes 12582912 | tf_op jit(solution)/shard_map/dot_general | solution.py:65
  343.4 12.2 %all-gather.11.cloned.1.call-done = bf16[2048,512]{0,1:T(8,128)(2,1)} async-done(((bf16[512,512]{0,1:T(8,128)(2,1)}), bf16[2048,512]{0,1:T(8,128)(2,1)}) %all-gather.11.cloned.1.call-update) | async-done | bytes 2097168 | tf_op jit(solution)/shard_map/all_gather | solution.py:63
  355.5 2.0 convert_reduce_fusion.1
  357.5 0.0 copy-start.3
  357.5 4.6 %convolution_reduce_fusion = f32[2048]{0:T(1024)S(1)} fusion(bf16[2048,2048]{1,0:T(8,128)(2,1)} %param.8, bf16[1,2048]{1,0:T(2,128)(2,1)S(1)} %get-tuple-element.7, bf16[1,2048]{1,0:T(2,128)(2,1)S(1)} %get-tuple-element.6, bf16[1,2048]{1,0:T(2,128)(2,1)S(1)} %convert_element_type.154), kind=kOutput, calls=%fused_computation.13 | convolution fusion | flops 25206784 | bytes 8409088 | tf_op jit(solution)/shard_map/dot_general | solution.py:74
  362.1 0.0 copy-done.3
  362.1 21.6 %psum.7 = f32[2048]{0:T(1024)S(1)} all-reduce(f32[2048]{0:T(1024)S(1)} %convolution_reduce_fusion), channel_id=1, replica_groups=mesh['lat'=8,'tok'=4] {'lat'}, use_global_device_ids=true, to_apply=%region_7.8 | all-reduce | flops 2048 | bytes 16384 | tf_op jit(solution)/shard_map/psum | solution.py:75
  383.8 0.6 sub.66
  384.4 8.4 %convolution_convert_fusion.1 = bf16[2048,2048]{1,0:T(8,128)(2,1)} fusion(bf16[2048,512]{0,1:T(8,128)(2,1)} %all-gather.11.cloned.1.call-done, bf16[2048,512]{0,1:T(8,128)(2,1)S(1)} %bitcast.45, f32[2048]{0:T(1024)S(1)} %dynamic-slice_convert_fusion), kind=kOutput, calls=%fused_computation.1 | convolution fusion | flops 4302307328 | bytes 12591104 | tf_op jit(solution)/shard_map/dot_general | solution.py:77
  (4 shorter events, 0.0 us)
Async XLA Ops:
  7.2 55.0 %all-gather.5.cloned.1.call-start = ((), (), s32[]{:S(2)}) async-start(), calls=%async_computation.4 | async-start | bytes 2359296 | tf_op jit(solution)/shard_map/all_gather | solution.py:36
  66.1 3.8 copy-start.5
  66.1 29.8 %all-to-all-start = ((bf16[4,2048,128]{1,2,0:T(8,128)(2,1)}), bf16[4,2048,128]{1,2,0:T(8,128)(2,1)S(1)}, u32[]{:S(2)}, u32[]{:S(2)}) async-start(bf16[4,2048,128]{1,2,0:T(8,128)(2,1)} %copy.15), calls=%async_computation | async-start | bytes 4194304 | tf_op jit(solution)/shard_map/all_to_all | solution.py:37
  69.8 65.3 %reduce-scatter.4.cloned.1.call-start = ((), (), s32[]{:S(2)}) async-start(), calls=%async_computation.5 | async-start | bytes 2621440 | tf_op jit(solution)/shard_map/reduce_scatter | solution.py:45
  95.9 9.9 %copy-start = (bf16[4,2048,128]{1,2,0:T(8,128)(2,1)}, bf16[4,2048,128]{1,2,0:T(8,128)(2,1)S(1)}, u32[]{:S(2)}) copy-start(bf16[4,2048,128]{1,2,0:T(8,128)(2,1)S(1)} %all-to-all-done) | copy-start | bytes 6291460
  105.8 0.8 copy-start.4
  105.8 54.1 %all-gather.7.cloned.1.call-start = ((), (), s32[]{:S(2)}) async-start(), calls=%async_computation.6 | async-start | bytes 2621440 | tf_op jit(solution)/shard_map/all_gather | solution.py:47
  137.2 101.1 %reduce-scatter.6.cloned.1.call-start = ((), (), s32[]{:S(2)}) async-start(), calls=%async_computation.7 | async-start | bytes 2359296 | tf_op jit(solution)/shard_map/reduce_scatter | solution.py:52
  169.8 68.5 %copy-start.1 = (bf16[4,2048,128]{1,2,0:T(8,128)(2,1)S(1)}, bf16[4,2048,128]{1,2,0:T(8,128)(2,1)}, u32[]{:S(2)}) copy-start(bf16[4,2048,128]{1,2,0:T(8,128)(2,1)} %copy-done) | copy-start | bytes 6291460
  169.8 121.3 %all-gather.9.cloned.1.call-start = ((), (), s32[]{:S(2)}) async-start(), calls=%async_computation.8 | async-start | bytes 2359296 | tf_op jit(solution)/shard_map/all_gather | solution.py:58
  240.0 90.7 %reduce-scatter.8.cloned.1.call-start = ((), (), s32[]{:S(2)}) async-start(), calls=%async_computation.9 | async-start | bytes 2621440 | tf_op jit(solution)/shard_map/reduce_scatter | solution.py:61
  301.0 54.6 %all-gather.11.cloned.1.call-start = ((), (), s32[]{:S(2)}) async-start(), calls=%async_computation.10 | async-start | bytes 2621440 | tf_op jit(solution)/shard_map/all_gather | solution.py:63
  332.8 2.2 copy-start.2
  357.5 4.6 %copy-start.3 = (f32[2048]{0:T(1024)}, f32[2048]{0:T(1024)S(1)}, u32[]{:S(2)}) copy-start(f32[2048]{0:T(1024)S(1)} %convert_reduce_fusion.1) | copy-start | bytes 24580
Sparse Core Ops, SparseCore 0:
  10.1 51.9 all-gather.4
  105.9 29.1 reduce-scatter.3
  137.3 22.5 all-gather.6
  169.9 68.2 reduce-scatter.5
  240.9 50.1 all-gather.8
  301.1 29.5 reduce-scatter.7
  332.9 22.5 all-gather.10
where the time goes:
time: 400 us
  waiting for transfers between devices  260 us (65%)
  blocking collectives  53.1 us (13%)
  matrix products  50.9 us (13%)
  between operations  14.3 us (4%)
  other arithmetic  11 us (3%)
  local copies, waits for them, and re-layouts  5.95 us (1%)
  starting transfers between devices  4.21 us (1%)
    reduce_scatter x1, waiting for transfers between devices, on_device(): recon = lax.psum_scatter(recon_part, 'lat', scatter_dimension=0, tiled=True)  68.3 us
    all_gather x1, waiting for transfers between devices, on_device(): resid_full = lax.all_gather(resid, 'lat', axis=0, tiled=True)  54.2 us
    all_gather x1, waiting for transfers between devices, on_device(): errors = lax.all_gather(error_rows, 'lat', axis=0, tiled=True)  51 us
    reduce_scatter x1, waiting for transfers between devices, on_device(): gc = lax.psum_scatter(gc_part, 'tok', scatter_dimension=0, tiled=True)  29.5 us
    all_gather x1, blocking collectives, on_device(): bias_full = lax.all_gather(b_dec, 'lat', axis=0, tiled=True)  26 us
    all_gather x1, waiting for transfers between devices, on_device(): codes = lax.all_gather(codes_rows, 'tok', axis=0, tiled=True)  22.7 us
    psum x1, blocking collectives, on_device(): back = lax.psum(back, 'lat')  21.6 us
    reduce_scatter x1, waiting for transfers between devices, on_device(): pre = lax.psum_scatter(pre_part, 'tok', scatter_dimension=0, tiled=True)  21.5 us
  transfers between devices with their start and end apart: 8, of which 7 were waited for; matrix products, arithmetic and copies ran while one was open for 3% of the time, Pallas kernels for 0%

commit v1 on v0

v1 whole, which is shorter than its diff:
```python
import functools

import jax
import jax.numpy as jnp
from jax import lax
from jax.experimental import pallas as pl
from jax.experimental.pallas import tpu as pltpu
from jax.sharding import PartitionSpec as P

f32 = jnp.float32
bf16 = jnp.bfloat16
MESH = pl.DeviceIdType.MESH
DMA = pltpu.SemaphoreType.DMA
VMEM = pltpu.VMEM


def remote(src, dst, send, recv, lat, tok):
    return pltpu.make_async_remote_copy(
        src_ref=src, dst_ref=dst, send_sem=send, recv_sem=recv,
        device_id=(lat, tok), device_id_type=MESH,
    )


def greet(devices):
    barrier = pltpu.get_barrier_semaphore()
    for lat, tok in devices:
        pl.semaphore_signal(barrier, inc=1, device_id=(lat, tok), device_id_type=MESH)
    pl.semaphore_wait(barrier, len(devices))


def column(lat, tok, count):
    return [(lax.rem(lat + s, count), tok) for s in range(1, count)]


def group(lat, tok, count):
    return [(lat, lax.rem(tok + s, count)) for s in range(1, count)]


def call(kernel, out_shape, inputs, scratch, ident, name):
    return pl.pallas_call(
        kernel,
        out_shape=out_shape,
        in_specs=[pl.BlockSpec(memory_space=VMEM)] * len(inputs),
        out_specs=pl.BlockSpec(memory_space=VMEM),
        scratch_shapes=scratch,
        compiler_params=pltpu.CompilerParams(
            collective_id=ident, has_side_effects=True, vmem_limit_bytes=40 * 2**20
        ),
        name=name,
    )(*inputs)


def spread_kernel(x_ref, out_ref, own_sem, first_send, up_send, down_send, side_send, recv):
    lat, tok = lax.axis_index("lat"), lax.axis_index("tok")
    z, y = lat // 2, lat % 2
    rows, cols = x_ref.shape
    greet(column(lat, tok, 8) + group(lat, tok, 4))

    def place(half, part):
        return out_ref.at[
            pl.ds(pl.multiple_of(half * rows, rows), rows),
            pl.ds(pl.multiple_of(part * cols, cols), cols),
        ]

    home = remote(x_ref, place(y, tok), first_send, recv.at[y * 4 + tok], lat, z)
    own = pltpu.make_async_copy(x_ref, place(y, tok), own_sem)

    @pl.when(tok != z)
    def _():
        home.start()

    @pl.when(tok == z)
    def _():
        own.start()

    goes_up = jnp.logical_and(z >= tok, z < 3)
    goes_down = jnp.logical_and(z <= tok, z > 0)
    moves = []
    for k in range(4):
        part = lax.rem(tok + k, 4)
        here = place(y, part)
        arrived = recv.at[y * 4 + part]
        up = remote(here, here, up_send.at[k], arrived, lat + 2, tok)
        down = remote(here, here, down_send.at[k], arrived, lat - 2, tok)
        side = remote(here, here, side_send.at[k], arrived, lat + 1 - 2 * y, tok)
        if k == 0:
            @pl.when(tok == z)
            def _():
                own.wait()

            @pl.when(tok != z)
            def _():
                side.wait_recv()
        else:
            side.wait_recv()

        @pl.when(goes_up)
        def _():
            up.start()

        @pl.when(goes_down)
        def _():
            down.start()

        side.start()
        moves.append((up, down, side))
    for k in range(4):
        part = lax.rem(tok + k, 4)
        there = place(1 - y, part)
        remote(there, there, side_send.at[k], recv.at[(1 - y) * 4 + part], lat, tok).wait_recv()
    for up, down, side in moves:
        @pl.when(goes_up)
        def _():
            up.wait_send()

        @pl.when(goes_down)
        def _():
            down.wait_send()

        side.wait_send()

    @pl.when(tok != z)
    def _():
        home.wait_send()


def spread(resid):
    rows, cols = resid.shape
    return call(
        spread_kernel,
        jax.ShapeDtypeStruct((2 * rows, 4 * cols), resid.dtype),
        (resid,),
        [DMA, DMA, DMA((4,)), DMA((4,)), DMA((4,)), DMA((8,))],
        1,
        "spread_features",
    )


def masked_sum_kernel(
    part_ref, bias_ref, active_ref, out_ref,
    near, sent, far, near_send, near_recv, far_send, far_recv,
    x_send, x_recv, c_send, c_recv, f_send, f_recv,
):
    lat, tok = lax.axis_index("lat"), lax.axis_index("tok")
    x, c = tok // 2, tok % 2
    ox, oc = 1 - x, 1 - c
    pair, across = x * 2 + oc, ox * 2 + c
    rows = part_ref.shape[1]
    half = rows // 2
    greet([(lat, pair), (lat, across)])

    swaps = []
    for n, bx in ((0, ox), (1, x)):
        swap = remote(
            part_ref.at[bx * 2 + oc], near.at[n], near_send.at[n], near_recv.at[n], lat, pair
        )
        swap.start()
        swaps.append(swap)
    swaps[0].wait_recv()
    cuts = [pl.ds(n * half, half) for n in range(2)]
    outs = []
    for n, cut in enumerate(cuts):
        sent[cut, :] = (
            part_ref[across, cut, :].astype(f32) + near[0, cut, :].astype(f32)
        ).astype(bf16)
        move = remote(
            sent.at[cut], far.at[cut], far_send.at[n], far_recv.at[n], lat, across
        )
        move.start()
        outs.append(move)
    swaps[1].wait_recv()
    gives = []
    for n, cut in enumerate(cuts):
        outs[n].wait_recv()
        total = (
            part_ref[tok, cut, :].astype(f32)
            + near[1, cut, :].astype(f32)
            + far[cut, :].astype(f32)
        )
        out_ref[tok, cut, :] = ((total + bias_ref[cut, :]) * active_ref[cut, :]).astype(bf16)
        mine = out_ref.at[tok, cut]
        for give in (
            remote(mine, mine, x_send.at[n], x_recv.at[n], lat, across),
            remote(mine, mine, c_send.at[n], c_recv.at[n], lat, pair),
        ):
            give.start()
            gives.append(give)
    for n, cut in enumerate(cuts):
        got = out_ref.at[across, cut]
        remote(got, got, x_send.at[n], x_recv.at[n], lat, across).wait_recv()
        give = remote(got, got, f_send.at[n], f_recv.at[n], lat, pair)
        give.start()
        gives.append(give)
    for n, cut in enumerate(cuts):
        got = out_ref.at[pair, cut]
        remote(got, got, c_send.at[n], c_recv.at[n], lat, pair).wait_recv()
        got = out_ref.at[ox * 2 + oc, cut]
        remote(got, got, f_send.at[n], f_recv.at[n], lat, pair).wait_recv()
    for move in swaps + outs + gives:
        move.wait_send()


def masked_sum(part, bias, active, ident):
    total, tokens = part.shape
    rows = total // 4
    return call(
        masked_sum_kernel,
        jax.ShapeDtypeStruct((4, rows, tokens), bf16),
        (part.reshape(4, rows, tokens), bias, active),
        [VMEM((2, rows, tokens), bf16), VMEM((rows, tokens), bf16), VMEM((rows, tokens), bf16)]
        + [DMA((2,))] * 10,
        ident,
        "masked_sum_%d" % ident,
    ).reshape(total, tokens)


def errors_kernel(
    part_ref, bias_ref, resid_ref, out_ref,
    side, below, above, sent,
    side_send, side_recv, line_send, below_recv, above_recv,
    up_send, down_send, turn_send, gather_recv,
):
    lat, tok = lax.axis_index("lat"), lax.axis_index("tok")
    z, y = lat // 2, lat % 2
    oy = 1 - y
    beside = z * 2 + oy
    greet(column(lat, tok, 8))
    high = z // 2
    order = (3 - 3 * high, 2 - high, 1 - z + 4 * high, z)

    swaps = []
    for d in order:
        swap = remote(
            part_ref.at[d * 2 + oy], side.at[d], side_send.at[d], side_recv.at[d], beside, tok
        )
        swap.start()
        swaps.append(swap)

    def held(d):
        return part_ref[d * 2 + y].astype(f32) + side[d].astype(f32)

    lines = []
    for d, swap in zip(order[:3], swaps[:3]):
        swap.wait_recv()
        up = remote(sent.at[d], below.at[d], line_send.at[d], below_recv.at[d], lat + 2, tok)
        down = remote(sent.at[d], above.at[d], line_send.at[d], above_recv.at[d], lat - 2, tok)
        sent[d] = held(d).astype(bf16)

        @pl.when(jnp.logical_and(d > z, z > 0))
        def _():
            up.wait_recv()
            sent[d] = (held(d) + below[d].astype(f32)).astype(bf16)

        @pl.when(jnp.logical_and(d < z, z < 3))
        def _():
            down.wait_recv()
            sent[d] = (held(d) + above[d].astype(f32)).astype(bf16)

        @pl.when(d > z)
        def _():
            up.start()

        @pl.when(d < z)
        def _():
            down.start()

        lines.append((d, up, down))
    swaps[3].wait_recv()

    from_below = remote(sent.at[z], below.at[z], line_send.at[z], below_recv.at[z], lat, tok)
    from_above = remote(sent.at[z], above.at[z], line_send.at[z], above_recv.at[z], lat, tok)

    def finish(total):
        out_ref[lat] = (total + bias_ref[...] - resid_ref[...].astype(f32)).astype(bf16)

    @pl.when(z == 0)
    def _():
        from_above.wait_recv()
        finish(held(z) + above[z].astype(f32))

    @pl.when(z == 3)
    def _():
        from_below.wait_recv()
        finish(held(z) + below[z].astype(f32))

    @pl.when(jnp.logical_and(z > 0, z < 3))
    def _():
        from_below.wait_recv()
        from_above.wait_recv()
        finish(held(z) + below[z].astype(f32) + above[z].astype(f32))

    def relay(o):
        here = out_ref.at[o * 2 + y]
        arrived = gather_recv.at[o * 2 + y]
        return (
            remote(here, here, up_send.at[o], arrived, lat + 2, tok),
            remote(here, here, down_send.at[o], arrived, lat - 2, tok),
            remote(here, here, turn_send.at[o], arrived, beside, tok),
        )

    up, down, turn = relay(z)
    pl.when(z < 3)(up.start)
    pl.when(z > 0)(down.start)
    turn.start()
    for s in range(1, 4):
        @pl.when(z - s >= 0)
        def _():
            up, down, turn = relay(z - s)
            turn.wait_recv()
            pl.when(z < 3)(up.start)
            turn.start()

        @pl.when(z + s <= 3)
        def _():
            up, down, turn = relay(z + s)
            turn.wait_recv()
            pl.when(z > 0)(down.start)
            turn.start()

    for o in range(4):
        there = out_ref.at[o * 2 + oy]
        remote(there, there, turn_send.at[o], gather_recv.at[o * 2 + oy], beside, tok).wait_recv()
    for o in range(4):
        up, down, turn = relay(o)
        pl.when(jnp.logical_and(o <= z, z < 3))(up.wait_send)
        pl.when(jnp.logical_and(o >= z, z > 0))(down.wait_send)
        turn.wait_send()
    for swap in swaps:
        swap.wait_send()
    for d, up, down in lines:
        up.wait_send()


def errors_of(part, bias, resid_rows):
    total, tokens = part.shape
    rows = total // 8
    return call(
        errors_kernel,
        jax.ShapeDtypeStruct((8, rows, tokens), bf16),
        (part.reshape(8, rows, tokens), bias, resid_rows),
        [VMEM((4, rows, tokens), bf16)] * 4 + [DMA((4,))] * 8 + [DMA((8,))],
        4,
        "recon_errors",
    ).reshape(total, tokens)


def small_sum_kernel(x_ref, out_ref, held, send, recv):
    lat, tok = lax.axis_index("lat"), lax.axis_index("tok")
    greet(column(lat, tok, 8))
    moves = []
    for s in range(1, 8):
        move = remote(
            x_ref, held.at[s], send.at[s], recv.at[s], lax.rem(lat + s, 8), tok
        )
        move.start()
        moves.append(move)
    held[0] = x_ref[...]
    for move in moves:
        move.wait_recv()
    out_ref[...] = jnp.sum(held[...], axis=0)
    for move in moves:
        move.wait_send()


def small_sum(x):
    wide = x.reshape(x.shape[0] // 128, 128)
    return call(
        small_sum_kernel,
        jax.ShapeDtypeStruct(wide.shape, f32),
        (wide,),
        [VMEM((8,) + wide.shape, f32), DMA((8,)), DMA((8,))],
        5,
        "small_sum",
    ).reshape(x.shape)


def active_rows(ids, base, rows):
    word = 32 if rows % 32 == 0 else rows
    local = ids - base
    which = local // word
    place = local - which * word
    bit = lax.shift_left(jnp.int32(1), place)
    words = lax.iota(jnp.int32, rows // word)
    held = jnp.where(which[None, :, :] == words[:, None, None], bit[None, :, :], 0)
    held = jnp.sum(held, axis=1)
    shifts = lax.iota(jnp.int32, word)
    flags = lax.shift_right_logical(held[:, None, :], jnp.broadcast_to(shifts[None, :, None], (rows // word, word, held.shape[1]))) & 1
    return flags.reshape(rows, held.shape[1]).astype(f32)


def on_device(kernels, resid, active_ids, w_enc, w_dec, b_enc, b_dec):
    block_rows = w_enc.shape[0]
    width = w_enc.shape[1]
    lat_pos = lax.axis_index("lat")
    tok_pos = lax.axis_index("tok")
    tok_count = lax.axis_size("tok")
    lat_count = lax.axis_size("lat")
    rows = block_rows // tok_count
    feats = width // lat_count

    ids_all = lax.all_gather(active_ids, "tok", axis=0, tiled=True).T
    bias_full = lax.all_gather(b_dec, "lat", axis=0, tiled=True)
    if kernels:
        resid_mine = spread(resid)
    else:
        resid_full = lax.all_gather(resid, "lat", axis=0, tiled=True)
        resid_mine = lax.all_to_all(resid_full, "tok", split_axis=0, concat_axis=1, tiled=True)
    bias_mine = lax.dynamic_slice_in_dim(bias_full, tok_pos * width, width, 0)
    centred = (resid_mine.astype(f32) - bias_mine.astype(f32)[:, None]).astype(bf16)

    active = active_rows(ids_all, lat_pos * block_rows + tok_pos * rows, rows)
    b_rows = lax.dynamic_slice_in_dim(b_enc, tok_pos * rows, rows, 0)

    pre_part = jnp.dot(w_enc, centred, preferred_element_type=f32).astype(bf16)
    if kernels:
        codes = masked_sum(pre_part, b_rows[:, None], active, 2)
    else:
        pre = lax.psum_scatter(pre_part.astype(f32), "tok", scatter_dimension=0, tiled=True)
        codes_rows = ((pre + b_rows[:, None]) * active).astype(bf16)
        codes = lax.all_gather(codes_rows, "tok", axis=0, tiled=True)

    recon_part = lax.dot_general(
        w_dec, codes, (((0,), (0,)), ((), ())), preferred_element_type=f32
    ).astype(bf16)
    r_rows = lax.dynamic_slice_in_dim(resid_mine, lat_pos * feats, feats, 0)
    bd_rows = lax.dynamic_slice_in_dim(bias_mine, lat_pos * feats, feats, 0)
    bd_rows = bd_rows.astype(f32)[:, None]
    if kernels:
        errors = errors_of(recon_part, bd_rows, r_rows)
    else:
        recon = lax.psum_scatter(
            recon_part.astype(f32), "lat", scatter_dimension=0, tiled=True
        )
        error_rows = (recon + bd_rows - r_rows.astype(f32)).astype(bf16)
        errors = lax.all_gather(error_rows, "lat", axis=0, tiled=True)

    gc_part = jnp.dot(w_dec, errors, preferred_element_type=f32).astype(bf16)
    if kernels:
        grad_pre = masked_sum(gc_part, jnp.zeros((rows, 1), f32), active, 3)
    else:
        gc = lax.psum_scatter(gc_part.astype(f32), "tok", scatter_dimension=0, tiled=True)
        gp_rows = (gc * active).astype(bf16)
        grad_pre = lax.all_gather(gp_rows, "tok", axis=0, tiled=True)

    grad_w_dec = lax.dot_general(
        codes, errors, (((1,), (1,)), ((), ())), preferred_element_type=f32
    ).astype(bf16)
    grad_b_enc = jnp.sum(grad_pre.astype(f32), axis=1)
    high = grad_b_enc.astype(bf16)
    rest = grad_b_enc - high.astype(f32)
    mid = rest.astype(bf16)
    low = (rest - mid.astype(f32)).astype(bf16)
    parts = jnp.stack([high, mid, low])
    back = jnp.sum(jnp.dot(parts, w_enc, preferred_element_type=f32), axis=0)
    back = small_sum(back) if kernels else lax.psum(back, "lat")
    error_total = jnp.sum(errors.astype(f32), axis=1)
    grad_w_enc = lax.dot_general(
        grad_pre, centred, (((1,), (1,)), ((), ())), preferred_element_type=f32
    ).astype(bf16)
    return (grad_w_enc, grad_w_dec, grad_b_enc, error_total - back)


def solution(mesh):
    kernels = mesh.shape["lat"] == 8 and mesh.shape["tok"] == 4
    return jax.shard_map(
        functools.partial(on_device, kernels),
        mesh=mesh,
        in_specs=(
            P("lat", "tok"),
            P("tok", None),
            P("lat", "tok"),
            P("lat", "tok"),
            P("lat"),
            P("lat"),
        ),
        out_specs=(P("lat", "tok"), P("lat", "tok"), P("lat"), P("tok")),
        check_vma=False,
    )
```

time: 400 us -> 260 us (0.65)
  waiting for transfers between devices: 260 us -> 0 us
  Pallas kernels: 0 us -> 159 us
  blocking collectives: 53.1 us -> 33.5 us
  between operations: 14.3 us -> 0.85 us
  local copies, waits for them, and re-layouts: 5.95 us -> 18.6 us
  other arithmetic: 11 us -> 1.93 us
  matrix products: 50.9 us -> 45.8 us
  starting transfers between devices: 4.21 us -> 0 us
    pallas_call x0 -> x5, Pallas kernels: none -> 159 us  [call(): pl.pallas_call(kernel, out_shape=out_shape, in_specs=[pl.BlockSpec(memory...]
    all_gather x4 -> x0, waiting for transfers between devices: 140 us -> none  [the longest x1 54.2 us: on_device(): resid_full = lax.all_gather(resid, 'lat', axis=0, tiled=True)]
    reduce_scatter x3 -> x0, waiting for transfers between devices: 119 us -> none  [the longest x1 68.3 us: on_device(): recon = lax.psum_scatter(recon_part, 'lat', scatter_dimension=0, tiled=True)]
    psum x1 -> x0, blocking collectives: 21.6 us -> none  [on_device(): back = lax.psum(back, 'lat')]
    convert_element_type x0 -> x3, local copies, waits for them, and re-layouts: none -> 9.28 us  [the longest x1 3.92 us: on_device(): gc_part = jnp.dot(w_dec, errors, preferred_element_type=f32).astype(bf16)]
    unnamed x12 -> x19, local copies, waits for them, and re-layouts: 0.71 us -> 7.35 us
    convert_element_type x4 -> x1, other arithmetic: 5.91 us -> 0.17 us  [active_rows(): return flags.reshape(rows, held.shape[1]).astype(f32)]
  transfers between devices with their start and end apart: 8 -> 0, of which waited for: 7 -> 0; matrix products, arithmetic and copies ran while one was open for 3% -> 0% of each run, Pallas kernels for 0% -> 0%
where the time goes in v1:
time: 260 us
  Pallas kernels  159 us (61%)
  matrix products  45.8 us (18%)
  blocking collectives  33.5 us (13%)
  local copies, waits for them, and re-layouts  18.6 us (7%)
    pallas_call x5, Pallas kernels, call(): pl.pallas_call(kernel, out_shape=out_shape, in_specs=[pl.BlockSpec(memory...  159 us
    all_gather x1, blocking collectives, on_device(): bias_full = lax.all_gather(b_dec, 'lat', axis=0, tiled=True)  27.9 us
    dot_general x1, matrix products, on_device(): pre_part = jnp.dot(w_enc, centred, preferred_element_type=f32).astype(bf16)  9.89 us
    dot_general x1, matrix products, on_device(): gc_part = jnp.dot(w_dec, errors, preferred_element_type=f32).astype(bf16)  9.3 us
    dot_general x1, matrix products, on_device(): lax.dot_general(w_dec, codes, (((0,), (0,)), ((), ())), preferred_element...  8.13 us
    unnamed x19, local copies, waits for them, and re-layouts  7.35 us
    dot_general x1, matrix products, on_device(): lax.dot_general(grad_pre, centred, (((1,), (1,)), ((), ())), preferred_el...  6.97 us
    dot_general x1, matrix products, on_device(): lax.dot_general(codes, errors, (((1,), (1,)), ((), ())), preferred_elemen...  6.78 us

profile of v1, /device:TPU:0, one launch (start us, length us, event | category | flops | bytes accessed | tf_op | source)
XLA Modules:
  0.0 259.6 jit_solution(14783839201331100345)
XLA Ops:
  0.6 0.0 copy-start.7
  0.7 0.8 dynamic_slice.15
  1.5 0.1 broadcast_in_dim.42
  1.5 27.9 %all_gather.6 = bf16[8192]{0:T(1024)(128)(2,1)S(1)} all-gather(bf16[1024]{0:T(1024)(128)(2,1)} %param.11), channel_id=1, replica_groups=mesh['lat'=8,'tok'=4] {'lat'}, dimensions={0}, use_global_device_ids=true | all-gather | bytes 18432 | tf_op jit(solution)/shard_map/all_gather | solution.py:402
  29.5 0.1 dynamic-slice_convert_fusion.1
  29.5 0.1 copy.26.bias_ref
  29.7 5.6 %all_gather.7 = s32[512,64]{0,1:T(8,128)S(1)} all-gather(s32[128,64]{0,1:T(8,128)} %param.7), channel_id=1, replica_groups=mesh['lat'=8,'tok'=4] {'tok'}, dimensions={0}, use_global_device_ids=true | all-gather | bytes 163840 | tf_op jit(solution)/shard_map/all_gather | solution.py:401
  35.3 0.1 add_select_fusion
  35.4 0.3 select_reduce_fusion
  35.7 0.9 copy.24.bias_ref
  36.5 0.2 fusion.4.active_ref
  36.7 0.0 copy-done.7
  36.7 21.3 %spread_features.1 = bf16[2048,512]{1,0:T(8,128)(2,1)S(1)} custom-call(bf16[1024,128]{1,0:T(8,128)(2,1)S(1)} %copy-done.7), custom_call_target="tpu_custom_call" | custom-call | tf_op jit(solution)/shard_map/spread_features/pallas_call | solution.py:40
  58.1 0.0 copy-start.2
  58.1 1.3 copy-done.2
  59.4 9.9 %fusion = bf16[2048,512]{0,1:T(8,128)(2,1)} fusion(bf16[2048,2048]{1,0:T(8,128)(2,1)} %param.8, bf16[2048,512]{1,0:T(8,128)(2,1)S(1)} %spread_features.1, f32[2048]{0:T(1024)S(1)} %dynamic-slice_convert_fusion), kind=kOutput, calls=%fused_computation.8 | convolution fusion | flops 4299161600 | bytes 12591104 | tf_op jit(solution)/shard_map/dot_general | solution.py:414
  69.3 2.9 %copy.23 = bf16[2048,512]{1,0:T(8,128)(2,1)S(1)} copy(bf16[2048,512]{0,1:T(8,128)(2,1)} %fusion) | data formatting | bytes 4194304 | tf_op jit(solution)/shard_map/convert_element_type | solution.py:414
  72.2 0.0 copy-start.6
  72.2 0.9 copy-done.6
  73.1 49.0 %masked_sum_2.1 = bf16[4,512,512]{2,1,0:T(8,128)(2,1)S(1)} custom-call(bf16[4,512,512]{2,1,0:T(8,128)(2,1)S(1)} %bitcast.65, f32[512,1]{1,0:T(8,128)S(1)} %copy-done.6, f32[512,512]{1,0:T(8,128)S(1)} %fusion.4.active_ref), custom_call_target="tpu_custom_call" | custom-call | tf_op jit(solution)/shard_map/masked_sum_2/pallas_call | solution.py:40
  122.1 0.0 copy-start.4
  122.1 1.3 copy-done.4
  123.4 8.1 %fusion.1 = bf16[2048,512]{0,1:T(8,128)(2,1)S(1)} fusion(bf16[2048,512]{1,0:T(8,128)(2,1)S(1)} %bitcast.66, bf16[2048,2048]{1,0:T(8,128)(2,1)} %param.9), kind=kOutput, calls=%fused_computation.9 | convolution fusion | flops 4296015872 | bytes 12582912 | tf_op jit(solution)/shard_map/dot_general | solution.py:422
  131.6 2.5 copy.25
  134.1 0.0 copy-start.1
  134.1 1.6 copy-done.1
  135.7 54.0 %recon_errors.1 = bf16[8,256,512]{2,1,0:T(8,128)(2,1)S(1)} custom-call(bf16[8,256,512]{2,1,0:T(8,128)(2,1)S(1)} %bitcast.64, f32[256,1]{1,0:T(8,128)S(1)} %copy.26.bias_ref, bf16[256,512]{1,0:T(8,128)(2,1)S(1)} %constant_dynamic-slice_fusion.resid_ref), custom_call_target="tpu_custom_call" | custom-call | tf_op jit(solution)/shard_map/recon_errors/pallas_call | solution.py:40
  189.6 0.3 convert_reduce_fusion
  190.0 9.3 %fusion.2 = bf16[2048,512]{0,1:T(8,128)(2,1)} fusion(bf16[2048,512]{1,0:T(8,128)(2,1)S(1)} %bitcast.60, bf16[2048,2048]{1,0:T(8,128)(2,1)} %param.9), kind=kOutput, calls=%fused_computation.10 | convolution fusion | flops 4296015872 | bytes 12582912 | tf_op jit(solution)/shard_map/dot_general | solution.py:437
  199.3 3.9 %copy.27 = bf16[2048,512]{1,0:T(8,128)(2,1)} copy(bf16[2048,512]{0,1:T(8,128)(2,1)} %fusion.2) | data formatting | bytes 4194304 | tf_op jit(solution)/shard_map/convert_element_type | solution.py:437
  203.2 0.0 copy-start
  203.2 1.6 copy-done
  204.8 27.2 %masked_sum_3.1 = bf16[4,512,512]{2,1,0:T(8,128)(2,1)S(1)} custom-call(bf16[4,512,512]{2,1,0:T(8,128)(2,1)S(1)} %bitcast.63, f32[512,1]{1,0:T(8,128)S(1)} %broadcast_in_dim.46.bias_ref, f32[512,512]{1,0:T(8,128)S(1)} %fusion.4.active_ref), custom_call_target="tpu_custom_call" | custom-call | tf_op jit(solution)/shard_map/masked_sum_3/pallas_call | solution.py:40
  232.0 0.4 convert_reduce_fusion.1
  232.3 0.6 copy.28
  233.0 0.0 copy-start.5
  233.0 4.7 %convolution_reduce_fusion = f32[2048]{0:T(1024)S(1)} fusion(bf16[2048,2048]{1,0:T(8,128)(2,1)} %param.8, bf16[1,2048]{1,0:T(2,128)(2,1)S(1)} %get-tuple-element.7, bf16[1,2048]{1,0:T(2,128)(2,1)S(1)} %get-tuple-element.6, bf16[1,2048]{1,0:T(2,128)(2,1)S(1)} %convert_element_type.125), kind=kOutput, calls=%fused_computation.13 | convolution fusion | flops 25206784 | bytes 8409088 | tf_op jit(solution)/shard_map/dot_general | solution.py:454
  237.8 7.4 %small_sum.1 = f32[16,128]{1,0:T(8,128)S(1)} custom-call(f32[16,128]{1,0:T(8,128)S(1)} %bitcast.68), custom_call_target="tpu_custom_call" | custom-call | tf_op jit(solution)/shard_map/small_sum/pallas_call | solution.py:40
  245.2 0.6 bitcast_subtract_fusion.1
  245.8 0.0 copy-done.5
  245.8 0.0 copy-start.3
  245.8 6.8 %convolution_convert_fusion = bf16[2048,2048]{1,0:T(8,128)(2,1)} fusion(bf16[2048,512]{1,0:T(8,128)(2,1)S(1)} %bitcast.67, bf16[2048,512]{1,0:T(8,128)(2,1)S(1)} %bitcast.61), kind=kOutput, calls=%fused_computation | convolution fusion | flops 4299161600 | bytes 12582912 | tf_op jit(solution)/shard_map/dot_general | solution.py:445
  252.6 0.0 copy-done.3
  252.6 7.0 %convolution_convert_fusion.1 = bf16[2048,2048]{1,0:T(8,128)(2,1)} fusion(bf16[2048,512]{1,0:T(8,128)(2,1)S(1)} %bitcast.62, bf16[2048,512]{1,0:T(8,128)(2,1)S(1)} %copy-done.3, f32[2048]{0:T(1024)S(1)} %dynamic-slice_convert_fusion), kind=kOutput, calls=%fused_computation.1 | convolution fusion | flops 4302307328 | bytes 12591104 | tf_op jit(solution)/shard_map/dot_general | solution.py:457
  (8 shorter events, 0.1 us)
Async XLA Ops:
  0.6 36.1 %copy-start.7 = (bf16[1024,128]{1,0:T(8,128)(2,1)S(1)}, bf16[1024,128]{1,0:T(8,128)(2,1)}, u32[]{:S(2)}) copy-start(bf16[1024,128]{1,0:T(8,128)(2,1)} %x_ref.1) | copy-start | bytes 786436
  58.1 1.4 copy-start.2
  72.2 1.0 copy-start.6
  122.1 1.3 copy-start.4
  134.1 1.6 copy-start.1
  203.2 1.6 copy-start
  233.0 12.8 %copy-start.5 = (bf16[4,512,512]{2,1,0:T(8,128)(2,1)S(1)}, bf16[4,512,512]{2,1,0:T(8,128)(2,1)}, u32[]{:S(2)}) copy-start(bf16[4,512,512]{2,1,0:T(8,128)(2,1)} %copy-done.4) | copy-start | bytes 6291460
  245.8 6.8 %copy-start.3 = (bf16[2048,512]{1,0:T(8,128)(2,1)S(1)}, bf16[2048,512]{1,0:T(8,128)(2,1)}, u32[]{:S(2)}) copy-start(bf16[2048,512]{1,0:T(8,128)(2,1)} %copy-done.2) | copy-start | bytes 6291460

commit v2 on v1

--- a/solution.py
+++ b/solution.py
@@ -36,109 +36,148 @@
     return [(lat, lax.rem(tok + s, count)) for s in range(1, count)]
 
 
-def call(kernel, out_shape, inputs, scratch, ident, name):
+def call(kernel, out_shape, inputs, scratch, ident, name, whole=()):
     return pl.pallas_call(
         kernel,
         out_shape=out_shape,
-        in_specs=[pl.BlockSpec(memory_space=VMEM)] * len(inputs),
-        out_specs=pl.BlockSpec(memory_space=VMEM),
+        in_specs=[
+            pl.BlockSpec(memory_space=pl.ANY if n in whole else VMEM)
+            for n in range(len(inputs))
+        ],
+        out_specs=jax.tree.map(lambda _: pl.BlockSpec(memory_space=VMEM), out_shape),
         scratch_shapes=scratch,
         compiler_params=pltpu.CompilerParams(
-            collective_id=ident, has_side_effects=True, vmem_limit_bytes=40 * 2**20
+            collective_id=ident, has_side_effects=True, vmem_limit_bytes=44 * 2**20
         ),
         name=name,
     )(*inputs)
 
 
-def spread_kernel(x_ref, out_ref, own_sem, first_send, up_send, down_send, side_send, recv):
+def spread_kernel(
+    x_ref, bias_ref, ids_ref, out_ref, bias_out, ids_out,
+    own_sem, first_send, up_send, down_send, side_send, recv,
+    bias_send, bias_recv, ids_send, ids_recv,
+):
     lat, tok = lax.axis_index("lat"), lax.axis_index("tok")
     z, y = lat // 2, lat % 2
     rows, cols = x_ref.shape
+    pieces = 2
+    cut = rows // pieces
     greet(column(lat, tok, 8) + group(lat, tok, 4))
 
-    def place(half, part):
+    def place(half, part, n):
         return out_ref.at[
-            pl.ds(pl.multiple_of(half * rows, rows), rows),
+            pl.ds(pl.multiple_of(half * rows + n * cut, cut), cut),
             pl.ds(pl.multiple_of(part * cols, cols), cols),
         ]
 
-    home = remote(x_ref, place(y, tok), first_send, recv.at[y * 4 + tok], lat, z)
-    own = pltpu.make_async_copy(x_ref, place(y, tok), own_sem)
-
-    @pl.when(tok != z)
-    def _():
-        home.start()
+    def sem_of(half, part, n):
+        return recv.at[half * (4 * pieces) + part * pieces + n]
+
+    firsts = []
+    for n in range(pieces):
+        mine = x_ref.at[pl.ds(n * cut, cut)]
+        home = remote(mine, place(y, tok, n), first_send.at[n], sem_of(y, tok, n), lat, z)
+        own = pltpu.make_async_copy(mine, place(y, tok, n), own_sem.at[n])
+        pl.when(tok != z)(home.start)
+        pl.when(tok == z)(own.start)
+        firsts.append((home, own))
+
+    bias_moves = [
+        remote(bias_ref, bias_out.at[y], bias_send.at[s], bias_recv.at[y], lax.rem(lat + s, 8), tok)
+        for s in range(1, 8)
+    ]
 
     @pl.when(tok == z)
     def _():
-        own.start()
+        for move in bias_moves:
+            move.start()
+        bias_out[y] = bias_ref[...]
+
+    def ids_place(part):
+        return ids_out.at[:, pl.ds(pl.multiple_of(part * cols, cols), cols)]
+
+    ids_moves = []
+    for s in range(1, 4):
+        move = remote(
+            ids_ref, ids_place(tok), ids_send.at[s], ids_recv.at[s], lat, lax.rem(tok + s, 4)
+        )
+        move.start()
+        ids_moves.append(move)
+    ids_out[:, pl.ds(pl.multiple_of(tok * cols, cols), cols)] = ids_ref[...]
 
     goes_up = jnp.logical_and(z >= tok, z < 3)
     goes_down = jnp.logical_and(z <= tok, z > 0)
     moves = []
     for k in range(4):
         part = lax.rem(tok + k, 4)
-        here = place(y, part)
-        arrived = recv.at[y * 4 + part]
-        up = remote(here, here, up_send.at[k], arrived, lat + 2, tok)
-        down = remote(here, here, down_send.at[k], arrived, lat - 2, tok)
-        side = remote(here, here, side_send.at[k], arrived, lat + 1 - 2 * y, tok)
-        if k == 0:
-            @pl.when(tok == z)
-            def _():
-                own.wait()
-
-            @pl.when(tok != z)
-            def _():
+        for n in range(pieces):
+            m = k * pieces + n
+            here = place(y, part, n)
+            arrived = sem_of(y, part, n)
+            up = remote(here, here, up_send.at[m], arrived, lat + 2, tok)
+            down = remote(here, here, down_send.at[m], arrived, lat - 2, tok)
+            side = remote(here, here, side_send.at[m], arrived, lat + 1 - 2 * y, tok)
+            if k == 0:
+                pl.when(tok == z)(firsts[n][1].wait)
+                pl.when(tok != z)(side.wait_recv)
+            else:
                 side.wait_recv()
-        else:
-            side.wait_recv()
-
-        @pl.when(goes_up)
-        def _():
-            up.start()
-
-        @pl.when(goes_down)
-        def _():
-            down.start()
-
-        side.start()
-        moves.append((up, down, side))
+            pl.when(goes_up)(up.start)
+            pl.when(goes_down)(down.start)
+            side.start()
+            moves.append((up, down, side))
     for k in range(4):
         part = lax.rem(tok + k, 4)
-        there = place(1 - y, part)
-        remote(there, there, side_send.at[k], recv.at[(1 - y) * 4 + part], lat, tok).wait_recv()
+        for n in range(pieces):
+            there = place(1 - y, part, n)
+            remote(
+                there, there, side_send.at[0], sem_of(1 - y, part, n), lat, tok
+            ).wait_recv()
+    for h in range(2):
+        @pl.when(jnp.logical_or(tok != z, y != h))
+        def _():
+            remote(
+                bias_ref, bias_out.at[h], bias_send.at[0], bias_recv.at[h], lat, tok
+            ).wait_recv()
+    for move in ids_moves:
+        move.wait_recv()
+        move.wait_send()
     for up, down, side in moves:
-        @pl.when(goes_up)
-        def _():
-            up.wait_send()
-
-        @pl.when(goes_down)
-        def _():
-            down.wait_send()
-
+        pl.when(goes_up)(up.wait_send)
+        pl.when(goes_down)(down.wait_send)
         side.wait_send()
-
-    @pl.when(tok != z)
+    for home, own in firsts:
+        pl.when(tok != z)(home.wait_send)
+
+    @pl.when(tok == z)
     def _():
-        home.wait_send()
-
-
-def spread(resid):
+        for move in bias_moves:
+            move.wait_send()
+
+
+def spread(resid, bias, ids):
     rows, cols = resid.shape
-    return call(
+    wide = bias.astype(f32).reshape(rows // 128, 128)
+    resid_mine, bias_mine, ids_all = call(
         spread_kernel,
-        jax.ShapeDtypeStruct((2 * rows, 4 * cols), resid.dtype),
-        (resid,),
-        [DMA, DMA, DMA((4,)), DMA((4,)), DMA((4,)), DMA((8,))],
+        (
+            jax.ShapeDtypeStruct((2 * rows, 4 * cols), resid.dtype),
+            jax.ShapeDtypeStruct((2,) + wide.shape, f32),
+            jax.ShapeDtypeStruct((ids.shape[1], 4 * cols), ids.dtype),
+        ),
+        (resid, wide, ids.T),
+        [DMA((2,)), DMA((2,)), DMA((8,)), DMA((8,)), DMA((8,)), DMA((16,))]
+        + [DMA((8,)), DMA((2,)), DMA((4,)), DMA((4,))],
         1,
         "spread_features",
     )
+    return resid_mine, bias_mine.reshape(2 * rows), ids_all
 
 
 def masked_sum_kernel(
-    part_ref, bias_ref, active_ref, out_ref,
-    near, sent, far, near_send, near_recv, far_send, far_recv,
+    w_ref, act_ref, bias_ref, active_ref, out_ref,
+    w, part_ref, w_sem, near, sent, far, near_send, near_recv, far_send, far_recv,
     x_send, x_recv, c_send, c_recv, f_send, f_recv,
 ):
     lat, tok = lax.axis_index("lat"), lax.axis_index("tok")
@@ -147,15 +186,35 @@
     pair, across = x * 2 + oc, ox * 2 + c
     rows = part_ref.shape[1]
     half = rows // 2
+    order = (ox * 2 + oc, pair, across, tok)
+    loads = []
+    for n, block in enumerate(order):
+        load = pltpu.make_async_copy(w_ref.at[block], w.at[n], w_sem.at[n])
+        load.start()
+        loads.append(load)
     greet([(lat, pair), (lat, across)])
+
+    def multiply(n):
+        loads[n].wait()
+
+        def step(m, carry):
+            cols = pl.ds(pl.multiple_of(m * 256, 256), 256)
+            part_ref[order[n], :, cols] = jnp.dot(
+                w[n], act_ref[:, cols], preferred_element_type=f32
+            ).astype(bf16)
+            return carry
+
+        lax.fori_loop(0, act_ref.shape[1] // 256, step, 0)
 
     swaps = []
     for n, bx in ((0, ox), (1, x)):
+        multiply(n)
         swap = remote(
             part_ref.at[bx * 2 + oc], near.at[n], near_send.at[n], near_recv.at[n], lat, pair
         )
         swap.start()
         swaps.append(swap)
+    multiply(2)
     swaps[0].wait_recv()
     cuts = [pl.ds(n * half, half) for n in range(2)]
     outs = []
@@ -168,6 +227,7 @@
         )
         move.start()
         outs.append(move)
+    multiply(3)
     swaps[1].wait_recv()
     gives = []
     for n, cut in enumerate(cuts):
@@ -200,23 +260,25 @@
         move.wait_send()
 
 
-def masked_sum(part, bias, active, ident):
-    total, tokens = part.shape
+def masked_sum(w, act, bias, active, ident):
+    total, tokens = w.shape[0], act.shape[1]
     rows = total // 4
     return call(
         masked_sum_kernel,
         jax.ShapeDtypeStruct((4, rows, tokens), bf16),
-        (part.reshape(4, rows, tokens), bias, active),
-        [VMEM((2, rows, tokens), bf16), VMEM((rows, tokens), bf16), VMEM((rows, tokens), bf16)]
+        (w.reshape(4, rows, w.shape[1]), act, bias, active),
+        [VMEM((4, rows, w.shape[1]), bf16), VMEM((4, rows, tokens), bf16), DMA((4,))]
+        + [VMEM((2, rows, tokens), bf16), VMEM((rows, tokens), bf16), VMEM((rows, tokens), bf16)]
         + [DMA((2,))] * 10,
         ident,
         "masked_sum_%d" % ident,
+        (0,),
     ).reshape(total, tokens)
 
 
 def errors_kernel(
-    part_ref, bias_ref, resid_ref, out_ref,
-    side, below, above, sent,
+    w_ref, codes_ref, bias_ref, resid_ref, out_ref,
+    w, part_ref, w_sem, side, below, above, sent,
     side_send, side_recv, line_send, below_recv, above_recv,
     up_send, down_send, turn_send, gather_recv,
 ):
@@ -224,12 +286,34 @@
     z, y = lat // 2, lat % 2
     oy = 1 - y
     beside = z * 2 + oy
-    greet(column(lat, tok, 8))
     high = z // 2
     order = (3 - 3 * high, 2 - high, 1 - z + 4 * high, z)
+    feats = part_ref.shape[1]
+    blocks = [d * 2 + oy for d in order] + [d * 2 + y for d in order]
+    loads = []
+    for n, block in enumerate(blocks):
+        load = pltpu.make_async_copy(
+            w_ref.at[:, pl.ds(pl.multiple_of(block * feats, feats), feats)], w.at[n], w_sem.at[n]
+        )
+        load.start()
+        loads.append(load)
+    greet(column(lat, tok, 8))
+
+    def multiply(n):
+        loads[n].wait()
+
+        def step(m, carry):
+            cols = pl.ds(pl.multiple_of(m * 256, 256), 256)
+            part_ref[blocks[n], :, cols] = lax.dot_general(
+                w[n], codes_ref[:, cols], (((0,), (0,)), ((), ())), preferred_element_type=f32
+            ).astype(bf16)
+            return carry
+
+        lax.fori_loop(0, codes_ref.shape[1] // 256, step, 0)
 
     swaps = []
-    for d in order:
+    for n, d in enumerate(order):
+        multiply(n)
         swap = remote(
             part_ref.at[d * 2 + oy], side.at[d], side_send.at[d], side_recv.at[d], beside, tok
         )
@@ -240,7 +324,8 @@
         return part_ref[d * 2 + y].astype(f32) + side[d].astype(f32)
 
     lines = []
-    for d, swap in zip(order[:3], swaps[:3]):
+    for n, (d, swap) in enumerate(zip(order[:3], swaps[:3])):
+        multiply(4 + n)
         swap.wait_recv()
         up = remote(sent.at[d], below.at[d], line_send.at[d], below_recv.at[d], lat + 2, tok)
         down = remote(sent.at[d], above.at[d], line_send.at[d], above_recv.at[d], lat - 2, tok)
@@ -265,6 +350,7 @@
             down.start()
 
         lines.append((d, up, down))
+    multiply(7)
     swaps[3].wait_recv()
 
     from_below = remote(sent.at[z], below.at[z], line_send.at[z], below_recv.at[z], lat, tok)
@@ -331,16 +417,18 @@
         up.wait_send()
 
 
-def errors_of(part, bias, resid_rows):
-    total, tokens = part.shape
+def errors_of(w, codes, bias, resid_rows):
+    total, tokens = w.shape[1], codes.shape[1]
     rows = total // 8
     return call(
         errors_kernel,
         jax.ShapeDtypeStruct((8, rows, tokens), bf16),
-        (part.reshape(8, rows, tokens), bias, resid_rows),
-        [VMEM((4, rows, tokens), bf16)] * 4 + [DMA((4,))] * 8 + [DMA((8,))],
+        (w, codes, bias, resid_rows),
+        [VMEM((8, w.shape[0], rows), bf16), VMEM((8, rows, tokens), bf16), DMA((8,))]
+        + [VMEM((4, rows, tokens), bf16)] * 4 + [DMA((4,))] * 8 + [DMA((8,))],
         4,
         "recon_errors",
+        (0,),
     ).reshape(total, tokens)
 
 
@@ -398,47 +486,45 @@
     rows = block_rows // tok_count
     feats = width // lat_count
 
-    ids_all = lax.all_gather(active_ids, "tok", axis=0, tiled=True).T
-    bias_full = lax.all_gather(b_dec, "lat", axis=0, tiled=True)
     if kernels:
-        resid_mine = spread(resid)
+        resid_mine, bias_mine, ids_all = spread(resid, b_dec, active_ids)
     else:
+        ids_all = lax.all_gather(active_ids, "tok", axis=0, tiled=True).T
+        bias_full = lax.all_gather(b_dec, "lat", axis=0, tiled=True)
         resid_full = lax.all_gather(resid, "lat", axis=0, tiled=True)
         resid_mine = lax.all_to_all(resid_full, "tok", split_axis=0, concat_axis=1, tiled=True)
-    bias_mine = lax.dynamic_slice_in_dim(bias_full, tok_pos * width, width, 0)
-    centred = (resid_mine.astype(f32) - bias_mine.astype(f32)[:, None]).astype(bf16)
+        bias_mine = lax.dynamic_slice_in_dim(bias_full, tok_pos * width, width, 0).astype(f32)
+    centred = (resid_mine.astype(f32) - bias_mine[:, None]).astype(bf16)
 
     active = active_rows(ids_all, lat_pos * block_rows + tok_pos * rows, rows)
     b_rows = lax.dynamic_slice_in_dim(b_enc, tok_pos * rows, rows, 0)
 
-    pre_part = jnp.dot(w_enc, centred, preferred_element_type=f32).astype(bf16)
     if kernels:
-        codes = masked_sum(pre_part, b_rows[:, None], active, 2)
+        codes = masked_sum(w_enc, centred, b_rows[:, None], active, 2)
     else:
-        pre = lax.psum_scatter(pre_part.astype(f32), "tok", scatter_dimension=0, tiled=True)
+        pre_part = jnp.dot(w_enc, centred, preferred_element_type=f32)
+        pre = lax.psum_scatter(pre_part, "tok", scatter_dimension=0, tiled=True)
         codes_rows = ((pre + b_rows[:, None]) * active).astype(bf16)
         codes = lax.all_gather(codes_rows, "tok", axis=0, tiled=True)
 
-    recon_part = lax.dot_general(
-        w_dec, codes, (((0,), (0,)), ((), ())), preferred_element_type=f32
-    ).astype(bf16)
     r_rows = lax.dynamic_slice_in_dim(resid_mine, lat_pos * feats, feats, 0)
     bd_rows = lax.dynamic_slice_in_dim(bias_mine, lat_pos * feats, feats, 0)
-    bd_rows = bd_rows.astype(f32)[:, None]
+    bd_rows = bd_rows[:, None]
     if kernels:
-        errors = errors_of(recon_part, bd_rows, r_rows)
+        errors = errors_of(w_dec, codes, bd_rows, r_rows)
     else:
-        recon = lax.psum_scatter(
-            recon_part.astype(f32), "lat", scatter_dimension=0, tiled=True
-        )
+        recon_part = lax.dot_general(
+            w_dec, codes, (((0,), (0,)), ((), ())), preferred_element_type=f32
+        )
+        recon = lax.psum_scatter(recon_part, "lat", scatter_dimension=0, tiled=True)
         error_rows = (recon + bd_rows - r_rows.astype(f32)).astype(bf16)
         errors = lax.all_gather(error_rows, "lat", axis=0, tiled=True)
 
-    gc_part = jnp.dot(w_dec, errors, preferred_element_type=f32).astype(bf16)
     if kernels:
-        grad_pre = masked_sum(gc_part, jnp.zeros((rows, 1), f32), active, 3)
+        grad_pre = masked_sum(w_dec, errors, jnp.zeros((rows, 1), f32), active, 3)
     else:
-        gc = lax.psum_scatter(gc_part.astype(f32), "tok", scatter_dimension=0, tiled=True)
+        gc_part = jnp.dot(w_dec, errors, preferred_element_type=f32)
+        gc = lax.psum_scatter(gc_part, "tok", scatter_dimension=0, tiled=True)
         gp_rows = (gc * active).astype(bf16)
         grad_pre = lax.all_gather(gp_rows, "tok", axis=0, tiled=True)
 

time: 260 us -> 190 us (0.73)
  blocking collectives: 33.5 us -> 0 us
  matrix products: 45.8 us -> 14.8 us
  local copies, waits for them, and re-layouts: 18.6 us -> 3.59 us
  Pallas kernels: 159 us -> 168 us
    all_gather x2 -> x0, blocking collectives: 33.5 us -> none  [the longest x1 27.9 us: on_device(): bias_full = lax.all_gather(b_dec, 'lat', axis=0, tiled=True)]
    dot_general x3 -> x0, matrix products: 27.3 us -> none  [the longest x1 9.89 us: on_device(): pre_part = jnp.dot(w_enc, centred, preferred_element_type=f32).astype(bf16)]
    convert_element_type x3 -> x0, local copies, waits for them, and re-layouts: 9.28 us -> none  [the longest x1 3.92 us: on_device(): gc_part = jnp.dot(w_dec, errors, preferred_element_type=f32).astype(bf16)]
    pallas_call x5, Pallas kernels: 159 us -> 168 us  [call(): pl.pallas_call(kernel, out_shape=out_shape, in_specs=[pl.BlockSpec(memory...]
    unnamed x19 -> x11, local copies, waits for them, and re-layouts: 7.35 us -> 2.34 us
    dot_general x1, matrix products: 4.73 us -> 1.2 us  [on_device(): back = jnp.sum(jnp.dot(parts, w_enc, preferred_element_type=f32), axis=0)]
where the time goes in v2:
time: 190 us
  Pallas kernels  168 us (88%)
  matrix products  14.8 us (8%)
  local copies, waits for them, and re-layouts  3.59 us (2%)
  other arithmetic  2.99 us (2%)
    pallas_call x5, Pallas kernels, call(): pl.pallas_call(kernel, out_shape=out_shape, in_specs=[pl.BlockSpec(memory...  168 us
    dot_general x1, matrix products, on_device(): lax.dot_general(codes, errors, (((1,), (1,)), ((), ())), preferred_elemen...  6.78 us
    dot_general x1, matrix products, on_device(): lax.dot_general(grad_pre, centred, (((1,), (1,)), ((), ())), preferred_el...  6.78 us

profile of v2, /device:TPU:0, one launch (start us, length us, event | category | flops | bytes accessed | tf_op | source)
XLA Modules:
  0.0 190.0 jit_solution(13664477821015935133)
XLA Ops:
  0.6 0.8 dynamic_slice.9
  1.4 0.7 bitcast_convert_fusion.bias_ref
  2.1 0.1 broadcast_in_dim.39
  2.2 0.1 copy.12.bias_ref
  2.3 0.0 copy-start
  2.3 0.9 copy-done
  3.3 0.0 copy-start.1
  3.3 0.8 copy-done.1
  4.0 28.8 %spread_features.1 = (bf16[2048,512]{1,0:T(8,128)(2,1)S(1)}, f32[2,8,128]{2,1,0:T(8,128)S(1)}, s32[64,512]{1,0:T(8,128)S(1)}) custom-call(bf16[1024,128]{1,0:T(8,128)(2,1)S(1)} %copy-done, f32[8,128]{1,0:T(8,128)S(1)} %bitcast_convert_fusion.bias_ref, s32[64,128]{1,0:T(8,128)S(1)} %bitcast.39), custom_call_target="tpu_custom_call" | custom-call | tf_op jit(solution)/shard_map/spread_features/pallas_call | solution.py:40
  32.8 0.1 dynamic_slice.10
  32.9 0.1 copy.13.bias_ref
  33.1 0.5 subtract_convert_fusion.act_ref
  33.5 0.1 add_select_fusion
  33.6 0.3 select_reduce_fusion
  33.9 0.2 fusion.1.active_ref
  34.1 42.5 %masked_sum_2.1 = bf16[4,512,512]{2,1,0:T(8,128)(2,1)S(1)} custom-call(bf16[4,512,2048]{2,1,0:T(8,128)(2,1)} %bitcast.42, bf16[2048,512]{1,0:T(8,128)(2,1)S(1)} %subtract_convert_fusion.act_ref, f32[512,1]{1,0:T(8,128)S(1)} %copy.12.bias_ref, f32[512,512]{1,0:T(8,128)S(1)} %fusion.1.active_ref), custom_call_target="tpu_custom_call" | custom-call | tf_op jit(solution)/shard_map/masked_sum_2/pallas_call | solution.py:40
  76.6 58.3 %recon_errors.1 = bf16[8,256,512]{2,1,0:T(8,128)(2,1)S(1)} custom-call(bf16[2048,2048]{1,0:T(8,128)(2,1)} %w_ref.1, bf16[2048,512]{1,0:T(8,128)(2,1)S(1)} %bitcast.35, f32[256,1]{1,0:T(8,128)S(1)} %copy.13.bias_ref, bf16[256,512]{1,0:T(8,128)(2,1)S(1)} %constant_dynamic-slice_fusion.resid_ref), custom_call_target="tpu_custom_call" | custom-call | tf_op jit(solution)/shard_map/recon_errors/pallas_call | solution.py:40
  134.8 0.0 slice-start
  134.9 0.3 convert_reduce_fusion
  135.3 0.0 slice-start.1
  135.3 31.7 %masked_sum_3.1 = bf16[4,512,512]{2,1,0:T(8,128)(2,1)S(1)} custom-call(bf16[4,512,2048]{2,1,0:T(8,128)(2,1)} %bitcast.45, bf16[2048,512]{1,0:T(8,128)(2,1)S(1)} %bitcast.33, f32[512,1]{1,0:T(8,128)S(1)} %broadcast_in_dim.42.bias_ref, f32[512,512]{1,0:T(8,128)S(1)} %fusion.1.active_ref), custom_call_target="tpu_custom_call" | custom-call | tf_op jit(solution)/shard_map/masked_sum_3/pallas_call | solution.py:40
  167.0 0.4 convert_reduce_fusion.1
  167.4 0.6 copy.14
  168.0 0.0 slice-done
  168.0 0.0 slice-done.1
  168.1 1.2 convolution_reduce_fusion
  169.3 6.6 %small_sum.1 = f32[16,128]{1,0:T(8,128)S(1)} custom-call(f32[16,128]{1,0:T(8,128)S(1)} %bitcast.38), custom_call_target="tpu_custom_call" | custom-call | tf_op jit(solution)/shard_map/small_sum/pallas_call | solution.py:40
  175.9 0.6 bitcast_subtract_fusion
  176.5 6.8 %convolution_convert_fusion = bf16[2048,2048]{1,0:T(8,128)(2,1)} fusion(bf16[2048,512]{1,0:T(8,128)(2,1)S(1)} %bitcast.36, bf16[2048,512]{1,0:T(8,128)(2,1)S(1)} %bitcast.34), kind=kOutput, calls=%fused_computation | convolution fusion | flops 4299161600 | bytes 12582912 | tf_op jit(solution)/shard_map/dot_general | solution.py:531
  183.2 6.8 %convolution_convert_fusion.1 = bf16[2048,2048]{1,0:T(8,128)(2,1)} fusion(bf16[2048,512]{1,0:T(8,128)(2,1)S(1)} %bitcast.37, bf16[2048,512]{1,0:T(8,128)(2,1)S(1)} %subtract_convert_fusion.act_ref), kind=kOutput, calls=%fused_computation.1 | convolution fusion | flops 4299161600 | bytes 12582912 | tf_op jit(solution)/shard_map/dot_general | solution.py:543
  (8 shorter events, 0.1 us)
Async XLA Ops:
  2.3 1.0 copy-start
  3.3 0.8 copy-start.1
  134.8 33.2 %slice-start = ((s8[8388608]{0:T(1024)(128)(4,1)}), s8[4194304]{0:T(1024)(128)(4,1)S(1)}, s32[]{:S(2)}) async-start(s8[8388608]{0:T(1024)(128)(4,1)} %bitcast.43), calls=%async_computation | async-start | bytes 8388608
  135.3 32.8 %slice-start.1 = ((s8[8388608]{0:T(1024)(128)(4,1)}), s8[4194304]{0:T(1024)(128)(4,1)S(1)}, s32[]{:S(2)}) async-start(s8[8388608]{0:T(1024)(128)(4,1)} %bitcast.43), calls=%async_computation.1 | async-start | bytes 8388608

commit v3 on v2

--- a/solution.py
+++ b/solution.py
@@ -299,122 +299,135 @@
         loads.append(load)
     greet(column(lat, tok, 8))
 
-    def multiply(n):
-        loads[n].wait()
-
-        def step(m, carry):
-            cols = pl.ds(pl.multiple_of(m * 256, 256), 256)
-            part_ref[blocks[n], :, cols] = lax.dot_general(
-                w[n], codes_ref[:, cols], (((0,), (0,)), ((), ())), preferred_element_type=f32
+    width = codes_ref.shape[1] // 2
+
+    def multiply(n, h):
+        if h == 0:
+            loads[n].wait()
+        cols = pl.ds(h * width, width)
+        part_ref[blocks[n], :, cols] = lax.dot_general(
+            w[n], codes_ref[:, cols], (((0,), (0,)), ((), ())), preferred_element_type=f32
+        ).astype(bf16)
+
+    swaps = []
+    for h in range(2):
+        cols = pl.ds(h * width, width)
+        for n, d in enumerate(order):
+            multiply(n, h)
+            swap = remote(
+                part_ref.at[d * 2 + oy, :, cols], side.at[d, :, cols],
+                side_send.at[h * 4 + d], side_recv.at[h * 4 + d], beside, tok,
+            )
+            swap.start()
+            swaps.append(swap)
+
+    lines = []
+
+    def reduce(h):
+        cols = pl.ds(h * width, width)
+
+        def held(d):
+            return part_ref[d * 2 + y, :, cols].astype(f32) + side[d, :, cols].astype(f32)
+
+        def chain(d):
+            m = h * 4 + d
+            src = sent.at[d, :, cols]
+            return (
+                remote(src, below.at[d, :, cols], line_send.at[m], below_recv.at[m], lat + 2, tok),
+                remote(src, above.at[d, :, cols], line_send.at[m], above_recv.at[m], lat - 2, tok),
+            )
+
+        for n, d in enumerate(order[:3]):
+            multiply(4 + n, h)
+            swaps[h * 4 + n].wait_recv()
+            up, down = chain(d)
+            sent[d, :, cols] = held(d).astype(bf16)
+
+            @pl.when(jnp.logical_and(d > z, z > 0))
+            def _():
+                up.wait_recv()
+                sent[d, :, cols] = (held(d) + below[d, :, cols].astype(f32)).astype(bf16)
+
+            @pl.when(jnp.logical_and(d < z, z < 3))
+            def _():
+                down.wait_recv()
+                sent[d, :, cols] = (held(d) + above[d, :, cols].astype(f32)).astype(bf16)
+
+            pl.when(d > z)(up.start)
+            pl.when(d < z)(down.start)
+            lines.append(up)
+        multiply(7, h)
+        swaps[h * 4 + 3].wait_recv()
+        from_below, from_above = chain(z)
+
+        def finish(total):
+            out_ref[lat, :, cols] = (
+                total + bias_ref[...] - resid_ref[:, cols].astype(f32)
             ).astype(bf16)
-            return carry
-
-        lax.fori_loop(0, codes_ref.shape[1] // 256, step, 0)
-
-    swaps = []
-    for n, d in enumerate(order):
-        multiply(n)
-        swap = remote(
-            part_ref.at[d * 2 + oy], side.at[d], side_send.at[d], side_recv.at[d], beside, tok
-        )
-        swap.start()
-        swaps.append(swap)
-
-    def held(d):
-        return part_ref[d * 2 + y].astype(f32) + side[d].astype(f32)
-
-    lines = []
-    for n, (d, swap) in enumerate(zip(order[:3], swaps[:3])):
-        multiply(4 + n)
-        swap.wait_recv()
-        up = remote(sent.at[d], below.at[d], line_send.at[d], below_recv.at[d], lat + 2, tok)
-        down = remote(sent.at[d], above.at[d], line_send.at[d], above_recv.at[d], lat - 2, tok)
-        sent[d] = held(d).astype(bf16)
-
-        @pl.when(jnp.logical_and(d > z, z > 0))
+
+        @pl.when(z == 0)
         def _():
-            up.wait_recv()
-            sent[d] = (held(d) + below[d].astype(f32)).astype(bf16)
-
-        @pl.when(jnp.logical_and(d < z, z < 3))
+            from_above.wait_recv()
+            finish(held(z) + above[z, :, cols].astype(f32))
+
+        @pl.when(z == 3)
         def _():
-            down.wait_recv()
-            sent[d] = (held(d) + above[d].astype(f32)).astype(bf16)
-
-        @pl.when(d > z)
+            from_below.wait_recv()
+            finish(held(z) + below[z, :, cols].astype(f32))
+
+        @pl.when(jnp.logical_and(z > 0, z < 3))
         def _():
-            up.start()
-
-        @pl.when(d < z)
-        def _():
-            down.start()
-
-        lines.append((d, up, down))
-    multiply(7)
-    swaps[3].wait_recv()
-
-    from_below = remote(sent.at[z], below.at[z], line_send.at[z], below_recv.at[z], lat, tok)
-    from_above = remote(sent.at[z], above.at[z], line_send.at[z], above_recv.at[z], lat, tok)
-
-    def finish(total):
-        out_ref[lat] = (total + bias_ref[...] - resid_ref[...].astype(f32)).astype(bf16)
-
-    @pl.when(z == 0)
-    def _():
-        from_above.wait_recv()
-        finish(held(z) + above[z].astype(f32))
-
-    @pl.when(z == 3)
-    def _():
-        from_below.wait_recv()
-        finish(held(z) + below[z].astype(f32))
-
-    @pl.when(jnp.logical_and(z > 0, z < 3))
-    def _():
-        from_below.wait_recv()
-        from_above.wait_recv()
-        finish(held(z) + below[z].astype(f32) + above[z].astype(f32))
-
-    def relay(o):
-        here = out_ref.at[o * 2 + y]
-        arrived = gather_recv.at[o * 2 + y]
+            from_below.wait_recv()
+            from_above.wait_recv()
+            finish(
+                held(z) + below[z, :, cols].astype(f32) + above[z, :, cols].astype(f32)
+            )
+
+    def relay(o, h):
+        here = out_ref.at[o * 2 + y, :, pl.ds(h * width, width)]
+        arrived = gather_recv.at[h * 8 + o * 2 + y]
+        m = h * 4 + o
         return (
-            remote(here, here, up_send.at[o], arrived, lat + 2, tok),
-            remote(here, here, down_send.at[o], arrived, lat - 2, tok),
-            remote(here, here, turn_send.at[o], arrived, beside, tok),
-        )
-
-    up, down, turn = relay(z)
-    pl.when(z < 3)(up.start)
-    pl.when(z > 0)(down.start)
-    turn.start()
-    for s in range(1, 4):
-        @pl.when(z - s >= 0)
-        def _():
-            up, down, turn = relay(z - s)
-            turn.wait_recv()
-            pl.when(z < 3)(up.start)
-            turn.start()
-
-        @pl.when(z + s <= 3)
-        def _():
-            up, down, turn = relay(z + s)
-            turn.wait_recv()
-            pl.when(z > 0)(down.start)
-            turn.start()
-
-    for o in range(4):
-        there = out_ref.at[o * 2 + oy]
-        remote(there, there, turn_send.at[o], gather_recv.at[o * 2 + oy], beside, tok).wait_recv()
-    for o in range(4):
-        up, down, turn = relay(o)
-        pl.when(jnp.logical_and(o <= z, z < 3))(up.wait_send)
-        pl.when(jnp.logical_and(o >= z, z > 0))(down.wait_send)
-        turn.wait_send()
-    for swap in swaps:
-        swap.wait_send()
-    for d, up, down in lines:
-        up.wait_send()
+            remote(here, here, up_send.at[m], arrived, lat + 2, tok),
+            remote(here, here, down_send.at[m], arrived, lat - 2, tok),
+            remote(here, here, turn_send.at[m], arrived, beside, tok),
+        )
+
+    for h in range(2):
+        reduce(h)
+        up, down, turn = relay(z, h)
+        pl.when(z < 3)(up.start)
+        pl.when(z > 0)(down.start)
+        turn.start()
+    for h in range(2):
+        for s in range(1, 4):
+            @pl.when(z - s >= 0)
+            def _():
+                up, down, turn = relay(z - s, h)
+                turn.wait_recv()
+                pl.when(z < 3)(up.start)
+                turn.start()
+
+            @pl.when(z + s <= 3)
+            def _():
+                up, down, turn = relay(z + s, h)
+                turn.wait_recv()
+                pl.when(z > 0)(down.start)
+                turn.start()
+
+    for h in range(2):
+        for o in range(4):
+            there = out_ref.at[o * 2 + oy, :, pl.ds(h * width, width)]
+            arrived = gather_recv.at[h * 8 + o * 2 + oy]
+            remote(there, there, turn_send.at[h * 4 + o], arrived, beside, tok).wait_recv()
+    for h in range(2):
+        for o in range(4):
+            up, down, turn = relay(o, h)
+            pl.when(jnp.logical_and(o <= z, z < 3))(up.wait_send)
+            pl.when(jnp.logical_and(o >= z, z > 0))(down.wait_send)
+            turn.wait_send()
+    for move in swaps + lines:
+        move.wait_send()
 
 
 def errors_of(w, codes, bias, resid_rows):
@@ -425,7 +438,7 @@
         jax.ShapeDtypeStruct((8, rows, tokens), bf16),
         (w, codes, bias, resid_rows),
         [VMEM((8, w.shape[0], rows), bf16), VMEM((8, rows, tokens), bf16), DMA((8,))]
-        + [VMEM((4, rows, tokens), bf16)] * 4 + [DMA((4,))] * 8 + [DMA((8,))],
+        + [VMEM((4, rows, tokens), bf16)] * 4 + [DMA((8,))] * 8 + [DMA((16,))],
         4,
         "recon_errors",
         (0,),

time: 190 us -> 192 us (1.011)
  Pallas kernels: 168 us -> 170 us
where the time goes in v3:
time: 192 us
  Pallas kernels  170 us (89%)
  matrix products  14.8 us (8%)
  local copies, waits for them, and re-layouts  3.59 us (2%)
  other arithmetic  2.99 us (2%)
    pallas_call x5, Pallas kernels, call(): pl.pallas_call(kernel, out_shape=out_shape, in_specs=[pl.BlockSpec(memory...  170 us
    dot_general x1, matrix products, on_device(): lax.dot_general(codes, errors, (((1,), (1,)), ((), ())), preferred_elemen...  6.78 us
    dot_general x1, matrix products, on_device(): lax.dot_general(grad_pre, centred, (((1,), (1,)), ((), ())), preferred_el...  6.78 us

profile of v3, /device:TPU:0, one launch (start us, length us, event | category | flops | bytes accessed | tf_op | source)
XLA Modules:
  0.0 191.9 jit_solution(7605317638524419829)
XLA Ops:
  0.6 0.8 dynamic_slice.9
  1.4 0.7 bitcast_convert_fusion.bias_ref
  2.1 0.1 broadcast_in_dim.39
  2.2 0.1 copy.12.bias_ref
  2.3 0.0 copy-start
  2.3 0.9 copy-done
  3.3 0.0 copy-start.1
  3.3 0.8 copy-done.1
  4.0 28.8 %spread_features.1 = (bf16[2048,512]{1,0:T(8,128)(2,1)S(1)}, f32[2,8,128]{2,1,0:T(8,128)S(1)}, s32[64,512]{1,0:T(8,128)S(1)}) custom-call(bf16[1024,128]{1,0:T(8,128)(2,1)S(1)} %copy-done, f32[8,128]{1,0:T(8,128)S(1)} %bitcast_convert_fusion.bias_ref, s32[64,128]{1,0:T(8,128)S(1)} %bitcast.39), custom_call_target="tpu_custom_call" | custom-call | tf_op jit(solution)/shard_map/spread_features/pallas_call | solution.py:40
  32.8 0.1 dynamic_slice.10
  32.9 0.1 copy.13.bias_ref
  33.1 0.5 subtract_convert_fusion.act_ref
  33.5 0.1 add_select_fusion
  33.6 0.3 select_reduce_fusion
  33.9 0.2 fusion.1.active_ref
  34.1 42.5 %masked_sum_2.1 = bf16[4,512,512]{2,1,0:T(8,128)(2,1)S(1)} custom-call(bf16[4,512,2048]{2,1,0:T(8,128)(2,1)} %bitcast.42, bf16[2048,512]{1,0:T(8,128)(2,1)S(1)} %subtract_convert_fusion.act_ref, f32[512,1]{1,0:T(8,128)S(1)} %copy.12.bias_ref, f32[512,512]{1,0:T(8,128)S(1)} %fusion.1.active_ref), custom_call_target="tpu_custom_call" | custom-call | tf_op jit(solution)/shard_map/masked_sum_2/pallas_call | solution.py:40
  76.6 60.5 %recon_errors.1 = bf16[8,256,512]{2,1,0:T(8,128)(2,1)S(1)} custom-call(bf16[2048,2048]{1,0:T(8,128)(2,1)} %w_ref.1, bf16[2048,512]{1,0:T(8,128)(2,1)S(1)} %bitcast.35, f32[256,1]{1,0:T(8,128)S(1)} %copy.13.bias_ref, bf16[256,512]{1,0:T(8,128)(2,1)S(1)} %constant_dynamic-slice_fusion.resid_ref), custom_call_target="tpu_custom_call" | custom-call | tf_op jit(solution)/shard_map/recon_errors/pallas_call | solution.py:40
  137.1 0.0 slice-start
  137.1 0.3 convert_reduce_fusion
  137.5 0.0 slice-start.1
  137.5 31.3 %masked_sum_3.1 = bf16[4,512,512]{2,1,0:T(8,128)(2,1)S(1)} custom-call(bf16[4,512,2048]{2,1,0:T(8,128)(2,1)} %bitcast.45, bf16[2048,512]{1,0:T(8,128)(2,1)S(1)} %bitcast.33, f32[512,1]{1,0:T(8,128)S(1)} %broadcast_in_dim.42.bias_ref, f32[512,512]{1,0:T(8,128)S(1)} %fusion.1.active_ref), custom_call_target="tpu_custom_call" | custom-call | tf_op jit(solution)/shard_map/masked_sum_3/pallas_call | solution.py:40
  168.9 0.4 convert_reduce_fusion.1
  169.2 0.6 copy.14
  169.9 0.0 slice-done
  169.9 0.0 slice-done.1
  169.9 1.2 convolution_reduce_fusion
  171.1 6.6 %small_sum.1 = f32[16,128]{1,0:T(8,128)S(1)} custom-call(f32[16,128]{1,0:T(8,128)S(1)} %bitcast.38), custom_call_target="tpu_custom_call" | custom-call | tf_op jit(solution)/shard_map/small_sum/pallas_call | solution.py:40
  177.7 0.6 bitcast_subtract_fusion
  178.3 6.8 %convolution_convert_fusion = bf16[2048,2048]{1,0:T(8,128)(2,1)} fusion(bf16[2048,512]{1,0:T(8,128)(2,1)S(1)} %bitcast.36, bf16[2048,512]{1,0:T(8,128)(2,1)S(1)} %bitcast.34), kind=kOutput, calls=%fused_computation | convolution fusion | flops 4299161600 | bytes 12582912 | tf_op jit(solution)/shard_map/dot_general | solution.py:544
  185.1 6.8 %convolution_convert_fusion.1 = bf16[2048,2048]{1,0:T(8,128)(2,1)} fusion(bf16[2048,512]{1,0:T(8,128)(2,1)S(1)} %bitcast.37, bf16[2048,512]{1,0:T(8,128)(2,1)S(1)} %subtract_convert_fusion.act_ref), kind=kOutput, calls=%fused_computation.1 | convolution fusion | flops 4299161600 | bytes 12582912 | tf_op jit(solution)/shard_map/dot_general | solution.py:556
  (8 shorter events, 0.1 us)
Async XLA Ops:
  2.3 1.0 copy-start
  3.3 0.8 copy-start.1
  137.1 32.8 %slice-start = ((s8[8388608]{0:T(1024)(128)(4,1)}), s8[4194304]{0:T(1024)(128)(4,1)S(1)}, s32[]{:S(2)}) async-start(s8[8388608]{0:T(1024)(128)(4,1)} %bitcast.43), calls=%async_computation | async-start | bytes 8388608
  137.5 32.4 %slice-start.1 = ((s8[8388608]{0:T(1024)(128)(4,1)}), s8[4194304]{0:T(1024)(128)(4,1)S(1)}, s32[]{:S(2)}) async-start(s8[8388608]{0:T(1024)(128)(4,1)} %bitcast.43), calls=%async_computation.1 | async-start | bytes 8388608

commit v4 on v2

--- a/solution.py
+++ b/solution.py
@@ -432,34 +432,11 @@
     ).reshape(total, tokens)
 
 
-def small_sum_kernel(x_ref, out_ref, held, send, recv):
-    lat, tok = lax.axis_index("lat"), lax.axis_index("tok")
-    greet(column(lat, tok, 8))
-    moves = []
-    for s in range(1, 8):
-        move = remote(
-            x_ref, held.at[s], send.at[s], recv.at[s], lax.rem(lat + s, 8), tok
-        )
-        move.start()
-        moves.append(move)
-    held[0] = x_ref[...]
-    for move in moves:
-        move.wait_recv()
-    out_ref[...] = jnp.sum(held[...], axis=0)
-    for move in moves:
-        move.wait_send()
-
-
 def small_sum(x):
-    wide = x.reshape(x.shape[0] // 128, 128)
-    return call(
-        small_sum_kernel,
-        jax.ShapeDtypeStruct(wide.shape, f32),
-        (wide,),
-        [VMEM((8,) + wide.shape, f32), DMA((8,)), DMA((8,))],
-        5,
-        "small_sum",
-    ).reshape(x.shape)
+    pair = x + lax.ppermute(x, "lat", [(n, n + 1 - 2 * (n % 2)) for n in range(8)])
+    return pair, [
+        lax.ppermute(pair, "lat", [(n, (n + s) % 8) for n in range(8)]) for s in (2, 4, 6)
+    ]
 
 
 def active_rows(ids, base, rows):
@@ -528,9 +505,6 @@
         gp_rows = (gc * active).astype(bf16)
         grad_pre = lax.all_gather(gp_rows, "tok", axis=0, tiled=True)
 
-    grad_w_dec = lax.dot_general(
-        codes, errors, (((1,), (1,)), ((), ())), preferred_element_type=f32
-    ).astype(bf16)
     grad_b_enc = jnp.sum(grad_pre.astype(f32), axis=1)
     high = grad_b_enc.astype(bf16)
     rest = grad_b_enc - high.astype(f32)
@@ -538,7 +512,15 @@
     low = (rest - mid.astype(f32)).astype(bf16)
     parts = jnp.stack([high, mid, low])
     back = jnp.sum(jnp.dot(parts, w_enc, preferred_element_type=f32), axis=0)
-    back = small_sum(back) if kernels else lax.psum(back, "lat")
+    if kernels:
+        back, others = small_sum(back)
+        codes, back = lax.optimization_barrier((codes, back))
+        back = back + (others[0] + others[1] + others[2])
+    else:
+        back = lax.psum(back, "lat")
+    grad_w_dec = lax.dot_general(
+        codes, errors, (((1,), (1,)), ((), ())), preferred_element_type=f32
+    ).astype(bf16)
     error_total = jnp.sum(errors.astype(f32), axis=1)
     grad_w_enc = lax.dot_general(
         grad_pre, centred, (((1,), (1,)), ((), ())), preferred_element_type=f32

time: 190 us -> 186 us (0.979)
  Pallas kernels: 168 us -> 161 us
  starting transfers between devices: 0 us -> 2.21 us
    pallas_call x5 -> x4, Pallas kernels: 168 us -> 161 us  [call(): pl.pallas_call(kernel, out_shape=out_shape, in_specs=[pl.BlockSpec(memory...]
    ppermute x0 -> x4, starting transfers between devices: none -> 2.21 us  [the longest x3 2.14 us: small_sum(): lax.ppermute(pair, 'lat', [(n, (n + s) % 8) for n in range(8)])]
  transfers between devices with their start and end apart: 0 -> 4, of which waited for: 0 -> 0; matrix products, arithmetic and copies ran while one was open for 0% -> 8% of each run, Pallas kernels for 0% -> 0%
where the time goes in v4:
time: 186 us; the launch traced here: 185 us
  Pallas kernels  161 us (87%)
  matrix products  14.8 us (8%)
  local copies, waits for them, and re-layouts  3.58 us (2%)
  other arithmetic  3 us (2%)
  starting transfers between devices  2.21 us (1%)
    pallas_call x4, Pallas kernels, call(): pl.pallas_call(kernel, out_shape=out_shape, in_specs=[pl.BlockSpec(memory...  161 us
    dot_general x1, matrix products, on_device(): lax.dot_general(grad_pre, centred, (((1,), (1,)), ((), ())), preferred_el...  6.8 us
    dot_general x1, matrix products, on_device(): lax.dot_general(codes, errors, (((1,), (1,)), ((), ())), preferred_elemen...  6.78 us
  transfers between devices with their start and end apart: 4, of which 0 were waited for; matrix products, arithmetic and copies ran while one was open for 8% of the time, Pallas kernels for 0%

profile of v4, /device:TPU:0, one launch (start us, length us, event | category | flops | bytes accessed | tf_op | source)
XLA Modules:
  0.0 185.4 jit_solution(5979982052571364622)
XLA Ops:
  0.6 0.7 bitcast_convert_fusion.bias_ref
  1.3 0.0 copy-start
  1.3 0.9 copy-done
  2.3 0.0 copy-start.1
  2.3 0.8 copy-done.1
  3.0 28.8 %spread_features.1 = (bf16[2048,512]{1,0:T(8,128)(2,1)S(1)}, f32[2,8,128]{2,1,0:T(8,128)S(1)}, s32[64,512]{1,0:T(8,128)S(1)}) custom-call(bf16[1024,128]{1,0:T(8,128)(2,1)S(1)} %copy-done, f32[8,128]{1,0:T(8,128)S(1)} %bitcast_convert_fusion.bias_ref, s32[64,128]{1,0:T(8,128)S(1)} %bitcast.35), custom_call_target="tpu_custom_call" | custom-call | tf_op jit(solution)/shard_map/spread_features/pallas_call | solution.py:40
  31.8 0.1 dynamic_slice.10
  31.9 0.5 subtract_convert_fusion.act_ref
  32.4 0.1 broadcast_in_dim.39
  32.5 0.8 dynamic_slice.9
  33.2 0.1 copy.12.bias_ref
  33.4 0.1 copy.13.bias_ref
  33.5 0.1 add_select_fusion
  33.6 0.3 select_reduce_fusion
  33.9 0.2 fusion.1.active_ref
  34.1 42.5 %masked_sum_2.1 = bf16[4,512,512]{2,1,0:T(8,128)(2,1)S(1)} custom-call(bf16[4,512,2048]{2,1,0:T(8,128)(2,1)} %bitcast.38, bf16[2048,512]{1,0:T(8,128)(2,1)S(1)} %subtract_convert_fusion.act_ref, f32[512,1]{1,0:T(8,128)S(1)} %copy.12.bias_ref, f32[512,512]{1,0:T(8,128)S(1)} %fusion.1.active_ref), custom_call_target="tpu_custom_call" | custom-call | tf_op jit(solution)/shard_map/masked_sum_2/pallas_call | solution.py:40
  76.6 0.0 slice-start
  76.6 58.2 %recon_errors.1 = bf16[8,256,512]{2,1,0:T(8,128)(2,1)S(1)} custom-call(bf16[2048,2048]{1,0:T(8,128)(2,1)} %w_ref.1, bf16[2048,512]{1,0:T(8,128)(2,1)S(1)} %bitcast.32, f32[256,1]{1,0:T(8,128)S(1)} %copy.13.bias_ref, bf16[256,512]{1,0:T(8,128)(2,1)S(1)} %constant_dynamic-slice_fusion.resid_ref), custom_call_target="tpu_custom_call" | custom-call | tf_op jit(solution)/shard_map/recon_errors/pallas_call | solution.py:40
  134.9 0.0 slice-start.1
  134.9 31.5 %masked_sum_3.1 = bf16[4,512,512]{2,1,0:T(8,128)(2,1)S(1)} custom-call(bf16[4,512,2048]{2,1,0:T(8,128)(2,1)} %bitcast.41, bf16[2048,512]{1,0:T(8,128)(2,1)S(1)} %bitcast.30, f32[512,1]{1,0:T(8,128)S(1)} %broadcast_in_dim.42.bias_ref, f32[512,512]{1,0:T(8,128)S(1)} %fusion.1.active_ref), custom_call_target="tpu_custom_call" | custom-call | tf_op jit(solution)/shard_map/masked_sum_3/pallas_call | solution.py:40
  166.3 0.4 convert_reduce_fusion.1
  166.8 0.0 slice-done
  166.8 0.0 slice-done.1
  166.8 1.2 convolution_reduce_fusion
  168.0 0.1 collective-permute-start
  168.1 6.8 %convolution_convert_fusion.1 = bf16[2048,2048]{1,0:T(8,128)(2,1)} fusion(bf16[2048,512]{1,0:T(8,128)(2,1)S(1)} %bitcast.34, bf16[2048,512]{1,0:T(8,128)(2,1)S(1)} %subtract_convert_fusion.act_ref), kind=kOutput, calls=%fused_computation.1 | convolution fusion | flops 4299161600 | bytes 12582912 | tf_op jit(solution)/shard_map/dot_general | solution.py:525
  174.9 0.3 convert_reduce_fusion
  175.2 0.6 copy.15
  175.8 0.0 collective-permute-done
  175.8 1.5 collective-permute-start.3
  177.3 0.0 collective-permute-start.2
  177.4 0.6 collective-permute-start.1
  178.0 6.8 %convolution_convert_fusion = bf16[2048,2048]{1,0:T(8,128)(2,1)} fusion(bf16[2048,512]{1,0:T(8,128)(2,1)S(1)} %bitcast.33, bf16[2048,512]{1,0:T(8,128)(2,1)S(1)} %bitcast.31), kind=kOutput, calls=%fused_computation | convolution fusion | flops 4299161600 | bytes 12582912 | tf_op jit(solution)/shard_map/dot_general | solution.py:521
  184.8 0.0 collective-permute-done.3
  184.8 0.0 collective-permute-done.2
  184.8 0.0 collective-permute-done.1
  184.8 0.6 add_subtract_fusion
  (9 shorter events, 0.1 us)
Async XLA Ops:
  1.3 0.9 copy-start
  2.3 0.8 copy-start.1
  76.6 90.2 %slice-start = ((s8[8388608]{0:T(1024)(128)(4,1)}), s8[4194304]{0:T(1024)(128)(4,1)S(1)}, s32[]{:S(2)}) async-start(s8[8388608]{0:T(1024)(128)(4,1)} %bitcast.39), calls=%async_computation | async-start | bytes 8388608
  134.9 31.9 %slice-start.1 = ((s8[8388608]{0:T(1024)(128)(4,1)}), s8[4194304]{0:T(1024)(128)(4,1)S(1)}, s32[]{:S(2)}) async-start(s8[8388608]{0:T(1024)(128)(4,1)} %bitcast.39), calls=%async_computation.1 | async-start | bytes 8388608
  168.0 7.8 %collective-permute-start = (f32[2048]{0:T(1024)S(1)}, f32[2048]{0:T(1024)S(1)}, u32[]{:S(2)}, u32[]{:S(2)}) collective-permute-start(f32[2048]{0:T(1024)S(1)} %convolution_reduce_fusion), channel_id=1, source_target_pairs={{0,4},{4,0},{8,12},{12,8},{16,20},{20,16},{24,28},{28,24},{1,5},{5... | collective-permute-start | bytes 24584 | tf_op jit(solution)/shard_map/ppermute | solution.py:436
  175.8 8.9 %collective-permute-start.3 = (f32[2048]{0:T(1024)S(1)}, f32[2048]{0:T(1024)S(1)}, u32[]{:S(2)}, u32[]{:S(2)}) collective-permute-start(f32[2048]{0:T(1024)S(1)} %add.26), channel_id=1, source_target_pairs={{0,24},{4,28},{8,0},{12,4},{16,8},{20,12},{24,16},{28,20},{1,25},{... | collective-permute-start | bytes 24584 | tf_op jit(solution)/shard_map/ppermute | solution.py:438
  177.3 7.4 %collective-permute-start.2 = (f32[2048]{0:T(1024)S(1)}, f32[2048]{0:T(1024)S(1)}, u32[]{:S(2)}, u32[]{:S(2)}) collective-permute-start(f32[2048]{0:T(1024)S(1)} %add.26), channel_id=1, source_target_pairs={{0,16},{4,20},{8,24},{12,28},{16,0},{20,4},{24,8},{28,12},{1,17},{... | collective-permute-start | bytes 24584 | tf_op jit(solution)/shard_map/ppermute | solution.py:438
  177.4 7.4 %collective-permute-start.1 = (f32[2048]{0:T(1024)S(1)}, f32[2048]{0:T(1024)S(1)}, u32[]{:S(2)}, u32[]{:S(2)}) collective-permute-start(f32[2048]{0:T(1024)S(1)} %add.26), channel_id=1, source_target_pairs={{0,8},{4,12},{8,16},{12,20},{16,24},{20,28},{24,0},{28,4},{1,9},{5... | collective-permute-start | bytes 24584 | tf_op jit(solution)/shard_map/ppermute | solution.py:438
